TPU v7x, 256 devices: a whole 4x4x8 slice. The times are simulated.
256 devices in a mesh: bead: 16 (over z, y_hi), space: 16 (over x, y_lo, core).
Axes of the slice: x: 4, y: 4 (y_hi: 2, y_lo: 2; y = y_hi * 2 + y_lo), z: 8, core: 2. Of those that a mesh axis runs over, the one named last changes fastest.
Arguments:
- features: bfloat16 [32, 16384, 128], P('bead', 'space'), may hold values from -6 to 6
- positions: float32 [32, 3, 16384], P('bead', None, 'space'), may hold values from 0 to 32, as said below
- send_rows: int32 [16, 2, 512], P('space'), may hold values from 0 to 1023
- neighbours: int32 [8, 16384], P(None, 'space'), may hold values from 0 to 2047
- nbr_mask: int32 [8, 16384], P(None, 'space'), may hold values 0 or 1
- w_pair: bfloat16 [128], replicated, may hold values from -0.5 to 0.5
- w_in: bfloat16 [256, 512], replicated, may hold values from -0.375 to 0.375
- w_out: bfloat16 [512, 128], replicated, may hold values from -0.25 to 0.25
- omega: float32 [32], P('bead'), may hold values from 0.1 to 1.5
- q_index: int32 [3, 64], replicated, may hold values from 1 to 4
Outputs:
- new_features: bfloat16 [32, 16384, 128], P('bead', 'space')
- new_positions: float32 [32, 3, 16384], P('bead', None, 'space')
- correlation: float32 [32, 32, 64], P('bead')
Inputs may be any that keep to these rules, and one draw needn't show every extreme that they name: `positions`: atom i of every bead has its first coordinate in [2 (i // 1024), 2 (i // 1024) + 2) and the other two in [0, 4).
All inputs are finite; a program needn't handle non-finite values. No bound on the sum of `nbr_mask` on one device may be relied on, other than what follows from the above.
Results may differ from a plain program's by a relative error of at most 0.0039.
Values may be sent and summed in bfloat16 or wider, within the bound.
A program may use at most 64 MiB of HBM per device.

v0:
```python
import math

import jax
import jax.numpy as jnp
from jax import lax
from jax.sharding import PartitionSpec as P


def with_halo(cells, sides, width):
    for axis, dim in sides:
        count = lax.axis_size(axis)
        head = lax.slice_in_dim(cells, 0, width, axis=dim)
        tail = lax.slice_in_dim(cells, cells.shape[dim] - width, cells.shape[dim], axis=dim)
        cells = jnp.concatenate(
            [
                lax.ppermute(tail, axis, [(i, (i + 1) % count) for i in range(count)]),
                cells,
                lax.ppermute(head, axis, [((i + 1) % count, i) for i in range(count)]),
            ],
            axis=dim,
        )
    return cells


def from_behind(block, axis, distance):
    devices = range(lax.axis_size(axis))
    route = [((i - distance) % len(devices), i) for i in devices]
    return lax.ppermute(block, axis, route)


def dct_table(order):
    kk = jnp.arange(order, dtype=jnp.float32)[:, None]
    bb = jnp.arange(order, dtype=jnp.float32)[None, :]
    scale = jnp.where(kk == 0, jnp.sqrt(1.0 / order), jnp.sqrt(2.0 / order)).astype(jnp.float32)
    return scale * jnp.cos(math.pi * kk * (bb + 0.5) / order)


def on_device(
    features, positions, send_rows, neighbours, nbr_mask, w_pair, w_in, w_out, omega, q_index
):
    per_dev, atoms_dev, width = features.shape
    ghost = send_rows.shape[2]
    nspace = lax.axis_size("space")
    nbead = lax.axis_size("bead")
    beads = per_dev * nbead
    box = 2.0 * nspace
    half = box / 2.0
    feat_rows = jnp.transpose(features, (1, 0, 2)).reshape(atoms_dev, per_dev * width)
    own_coords = jnp.transpose(positions, (2, 0, 1))
    coord_rows = own_coords.reshape(atoms_dev, per_dev * 3)
    send_index = jnp.concatenate([send_rows[0, 0], send_rows[0, 1]], axis=0)
    outgoing = jnp.take(feat_rows, send_index, axis=0)
    coords_out = jnp.take(coord_rows, send_index, axis=0)
    padded = with_halo(outgoing, (("space", 0),), ghost)
    coords_pad = with_halo(coords_out, (("space", 0),), ghost)
    below_coords = coords_pad[:ghost]
    above_coords = coords_pad[-ghost:]
    extended = jnp.concatenate([feat_rows, padded[:ghost], padded[-ghost:]], axis=0)
    ext_rows = extended.shape[0]
    ext_coords = jnp.concatenate([coord_rows, below_coords, above_coords], axis=0)
    strength = jnp.einsum(
        "rbw,w->rb",
        extended.reshape(ext_rows, per_dev, width),
        w_pair,
        preferred_element_type=jnp.float32,
    )
    small_table = jnp.concatenate([ext_coords, strength], axis=1)
    own_strength = strength[:atoms_dev]
    maskf = nbr_mask.astype(jnp.float32)
    agg = jnp.zeros((atoms_dev, per_dev, width), jnp.float32)
    force = jnp.zeros((atoms_dev, per_dev, 3), jnp.float32)
    for slot in range(neighbours.shape[0]):
        idx = neighbours[slot]
        rows = jnp.take(extended, idx, axis=0).reshape(atoms_dev, per_dev, width)
        picked = jnp.take(small_table, idx, axis=0)
        other = picked[:, : per_dev * 3].reshape(atoms_dev, per_dev, 3)
        other_strength = picked[:, per_dev * 3 :]
        delta = own_coords - other
        first = delta[:, :, 0]
        first = jnp.where(first > half, first - box, jnp.where(first < -half, first + box, first))
        delta = jnp.concatenate([first[:, :, None], delta[:, :, 1:]], axis=2)
        dist_sq = jnp.sum(delta * delta, axis=2)
        weight = maskf[slot][:, None] / (1.0 + dist_sq / 4.0)
        agg = agg + weight[:, :, None] * rows.astype(jnp.float32)
        pair = weight * (own_strength + other_strength)
        force = force + pair[:, :, None] * delta
    agg_beads = jnp.transpose(agg.astype(jnp.bfloat16), (1, 0, 2))
    force = jnp.transpose(force, (1, 2, 0))
    joined = jnp.concatenate([features, agg_beads], axis=2)
    hidden = jax.nn.silu(
        jnp.einsum("bai,ih->bah", joined, w_in, preferred_element_type=jnp.float32)
    ).astype(jnp.bfloat16)
    new_features = (
        features.astype(jnp.float32)
        + jnp.einsum("bah,hw->baw", hidden, w_out, preferred_element_type=jnp.float32)
    ).astype(jnp.bfloat16)
    table = dct_table(beads)
    group = lax.axis_index("bead")
    first_bead = group * per_dev
    stacked = jnp.concatenate([positions, force], axis=1)
    piece = lax.all_gather(stacked, "bead", axis=0, tiled=True)
    block = lax.dynamic_slice(table, (first_bead, 0), (per_dev, piece.shape[0]))
    modes = jnp.einsum("kb,bca->kca", block, piece, precision=lax.Precision.HIGHEST)
    rotated = (
        jnp.cos(omega)[:, None, None] * modes[:, :3] + jnp.sin(omega)[:, None, None] * modes[:, 3:]
    )
    piece = lax.all_gather(rotated, "bead", axis=0, tiled=True)
    block = lax.dynamic_slice(table, (0, first_bead), (piece.shape[0], per_dev))
    new_positions = jnp.einsum("kb,kca->bca", block, piece, precision=lax.Precision.HIGHEST)
    lengths = jnp.array([box, 4.0, 4.0], dtype=jnp.float32)
    qvec = 2.0 * math.pi * q_index.astype(jnp.float32) / lengths[:, None]
    phase = jnp.einsum("cq,bca->bqa", qvec, new_positions, precision=lax.Precision.HIGHEST)
    partial_sums = jnp.stack(
        [jnp.sum(jnp.cos(phase), axis=2), jnp.sum(jnp.sin(phase), axis=2)], axis=1
    )
    sfac = lax.psum(partial_sums, "space")
    atoms_total = float(atoms_dev * nspace)
    local_ids = first_bead + jnp.arange(per_dev, dtype=jnp.int32)
    lags = jnp.arange(beads, dtype=jnp.int32)

    def place(out, remote, source):
        remote_ids = source * per_dev + jnp.arange(per_dev, dtype=jnp.int32)
        lag_of = (remote_ids[None, :] - local_ids[:, None]) % beads
        values = (
            jnp.einsum("bcq,jcq->bjq", sfac, remote, precision=lax.Precision.HIGHEST) / atoms_total
        )
        hit = lag_of[:, :, None] == lags[None, None, :]
        filled = jnp.any(hit, axis=1)
        placed = jnp.einsum(
            "bjt,bjq->btq", hit.astype(jnp.float32), values, precision=lax.Precision.HIGHEST
        )
        return jnp.where(filled[:, :, None], placed, out)

    start_out = jnp.zeros((per_dev, beads, sfac.shape[2]), jnp.float32)

    def loop_step(turn, carry):
        current, out = carry
        current = from_behind(current, "bead", 1)
        return (current, place(out, current, (group - turn) % nbead))

    _, correlation = lax.fori_loop(1, nbead, loop_step, (sfac, place(start_out, sfac, group)))
    return (new_features, new_positions, correlation)


def solution(mesh):
    in_specs = (
        P("bead", "space", None),
        P("bead", None, "space"),
        P("space", None, None),
        P(None, "space"),
        P(None, "space"),
        P(),
        P(),
        P(),
        P("bead"),
        P(),
    )
    out_specs = (P("bead", "space", None), P("bead", None, "space"), P("bead", None, None))
    return jax.shard_map(
        on_device, mesh=mesh, in_specs=in_specs, out_specs=out_specs, check_vma=False
    )
```

profile of v0, /device:TPU:0, one launch (start us, length us, event | category | flops | bytes accessed | tf_op | source)
XLA Modules:
  0.0 459.8 jit_solution(1415022534163254387)
XLA Ops:
  2.5 3.9 gather_fusion.1
  13.2 3.9 collective-permute-start.2
  77.7 49.5 %all_gather.6 = f32[32,6,1024]{2,1,0:T(8,128)S(1)} all-gather(f32[2,6,1024]{2,1,0:T(8,128)S(1)} %pad_maximum_fusion.1), channel_id=1, replica_groups=mesh['bead'=16,'space'=16] {'bead'}, dimensions={0}, use_global_device_ids=true | all-gather | bytes 835584 | tf_op jit(solution)/shard_map/all_gather | solution.py:101
  128.2 41.0 %all_gather.7 = f32[32,3,1024]{2,1,0:T(4,128)S(1)} all-gather(f32[2,3,1024]{2,1,0:T(4,128)S(1)} %copy.512), channel_id=1, replica_groups=mesh['bead'=16,'space'=16] {'bead'}, dimensions={0}, use_global_device_ids=true | all-gather | bytes 417792 | tf_op jit(solution)/shard_map/all_gather | solution.py:107
  169.8 3.7 cosine_reduce_fusion
  173.9 53.1 %psum.7 = f32[2,2,64]{1,0,2:T(2,128)S(1)} all-reduce(f32[2,2,64]{1,0,2:T(2,128)S(1)} %pad_maximum_fusion.2), channel_id=1, replica_groups=mesh['bead'=16,'space'=16] {'space'}, use_global_device_ids=true, to_apply=%region_10.13 | all-reduce | flops 256 | bytes 2048 | tf_op jit(solution)/shard_map/psum | solution.py:116
  227.7 3.9 gather_fusion.3
  231.7 5.0 %gather_fusion.5 = bf16[1024,256]{1,0:T(8,128)(2,1)} fusion(bf16[2048,256]{1,0:T(8,128)(2,1)S(1)} %constant_dynamic-update-slice_fusion, s32[1024]{0:T(1024)S(1)} %copy-done.14), kind=kCustom, calls=%fused_computation.9.clone | custom fusion | bytes 1052672 | tf_op jit(solution)/shard_map/jit(_take)/gather | solution.py:74
  236.7 5.0 %gather_fusion.7 = bf16[1024,256]{1,0:T(8,128)(2,1)} fusion(bf16[2048,256]{1,0:T(8,128)(2,1)S(1)} %constant_dynamic-update-slice_fusion, s32[1024]{0:T(1024)S(1)} %copy-done.18), kind=kCustom, calls=%fused_computation.10.clone | custom fusion | bytes 1052672 | tf_op jit(solution)/shard_map/jit(_take)/gather | solution.py:74
  241.7 5.0 %gather_fusion.9 = bf16[1024,256]{1,0:T(8,128)(2,1)} fusion(bf16[2048,256]{1,0:T(8,128)(2,1)S(1)} %constant_dynamic-update-slice_fusion, s32[1024]{0:T(1024)S(1)} %copy-done.17), kind=kCustom, calls=%fused_computation.11.clone | custom fusion | bytes 1052672 | tf_op jit(solution)/shard_map/jit(_take)/gather | solution.py:74
  246.6 5.0 %gather_fusion.11 = bf16[1024,256]{1,0:T(8,128)(2,1)} fusion(bf16[2048,256]{1,0:T(8,128)(2,1)S(1)} %constant_dynamic-update-slice_fusion, s32[1024]{0:T(1024)S(1)} %copy-done.20), kind=kCustom, calls=%fused_computation.12.clone | custom fusion | bytes 1052672 | tf_op jit(solution)/shard_map/jit(_take)/gather | solution.py:74
  251.6 5.0 %gather_fusion.13 = bf16[1024,256]{1,0:T(8,128)(2,1)} fusion(bf16[2048,256]{1,0:T(8,128)(2,1)S(1)} %constant_dynamic-update-slice_fusion, s32[1024]{0:T(1024)S(1)} %copy-done.19), kind=kCustom, calls=%fused_computation.13.clone | custom fusion | bytes 1052672 | tf_op jit(solution)/shard_map/jit(_take)/gather | solution.py:74
  256.6 5.0 %gather_fusion.15 = bf16[1024,256]{1,0:T(8,128)(2,1)} fusion(bf16[2048,256]{1,0:T(8,128)(2,1)S(1)} %constant_dynamic-update-slice_fusion, s32[1024]{0:T(1024)S(1)} %copy-done.22), kind=kCustom, calls=%fused_computation.14.clone | custom fusion | bytes 1052672 | tf_op jit(solution)/shard_map/jit(_take)/gather | solution.py:74
  261.6 3.9 gather_fusion.17
  315.2 6.1 %fusion.28 = bf16[2,1024,128]{2,1,0:T(8,128)(2,1)S(1)} fusion(f32[1024,2,128]{2,0,1:T(8,128)} %copy.509, f32[1024,2]{0,1:T(2,128)} %get-tuple-element.309, f32[1024,2,128]{2,0,1:T(8,128)} %copy.505, f32[1024,2]{0,1:T(2,128)} %get-tuple-element.307, f32[1024,2,128]{2,0,1:T(8,128)} %copy.501, f32[1024,2]{0,1:T(2,128)} %get-tuple-element.305, ...), kind=kLoop, calls=%fused_computation.66 | loop fusion | flops 4194304 | bytes 8978432 | tf_op jit(solution)/shard_map/transpose | solution.py:87
  321.3 3.4 fusion.12
  324.7 134.4 %while.19 = (s32[]{:T(128)}, f32[2,2,64]{1,0,2:T(2,128)S(1)}, f32[2,32,64]{2,1,0:T(8,128)S(1)}, s32[]{:T(128)}, f32[2,2,64]{1,0,2:T(2,128)S(1)}, /*index=5*/s32[...) while((s32[]{:T(128)}, f32[2,2,64]{1,0,2:T(2,128)S(1)}, ...), condition=%wide.region_14.17_spmd.clone, body=%wide.region_12.16_spmd.clone.sunk | while | flops 109187 | bytes 45554 | solution.py:141
  326.0 6.5 %collective-permute-done = f32[2,2,64]{1,0,2:T(2,128)S(1)} collective-permute-done((f32[2,2,64]{1,0,2:T(2,128)S(1)}, f32[2,2,64]{1,0,2:T(2,128)S(1)}, u32[]{:S(2)}, u32[]{:S(2)}) %collective-permute-start) | collective-permute-done | bytes 1056 | tf_op jit(solution)/shard_map/while/body/eval_jaxpr/ppermute | solution.py:28
  333.9 7.7 %collective-permute-done = f32[2,2,64]{1,0,2:T(2,128)S(1)} collective-permute-done((f32[2,2,64]{1,0,2:T(2,128)S(1)}, f32[2,2,64]{1,0,2:T(2,128)S(1)}, u32[]{:S(2)}, u32[]{:S(2)}) %collective-permute-start) | collective-permute-done | bytes 1056 | tf_op jit(solution)/shard_map/while/body/eval_jaxpr/ppermute | solution.py:28
  342.8 7.8 %collective-permute-done = f32[2,2,64]{1,0,2:T(2,128)S(1)} collective-permute-done((f32[2,2,64]{1,0,2:T(2,128)S(1)}, f32[2,2,64]{1,0,2:T(2,128)S(1)}, u32[]{:S(2)}, u32[]{:S(2)}) %collective-permute-start) | collective-permute-done | bytes 1056 | tf_op jit(solution)/shard_map/while/body/eval_jaxpr/ppermute | solution.py:28
  351.9 7.7 %collective-permute-done = f32[2,2,64]{1,0,2:T(2,128)S(1)} collective-permute-done((f32[2,2,64]{1,0,2:T(2,128)S(1)}, f32[2,2,64]{1,0,2:T(2,128)S(1)}, u32[]{:S(2)}, u32[]{:S(2)}) %collective-permute-start) | collective-permute-done | bytes 1056 | tf_op jit(solution)/shard_map/while/body/eval_jaxpr/ppermute | solution.py:28
  360.9 7.7 %collective-permute-done = f32[2,2,64]{1,0,2:T(2,128)S(1)} collective-permute-done((f32[2,2,64]{1,0,2:T(2,128)S(1)}, f32[2,2,64]{1,0,2:T(2,128)S(1)}, u32[]{:S(2)}, u32[]{:S(2)}) %collective-permute-start) | collective-permute-done | bytes 1056 | tf_op jit(solution)/shard_map/while/body/eval_jaxpr/ppermute | solution.py:28
  369.8 7.7 %collective-permute-done = f32[2,2,64]{1,0,2:T(2,128)S(1)} collective-permute-done((f32[2,2,64]{1,0,2:T(2,128)S(1)}, f32[2,2,64]{1,0,2:T(2,128)S(1)}, u32[]{:S(2)}, u32[]{:S(2)}) %collective-permute-start) | collective-permute-done | bytes 1056 | tf_op jit(solution)/shard_map/while/body/eval_jaxpr/ppermute | solution.py:28
  378.8 7.7 %collective-permute-done = f32[2,2,64]{1,0,2:T(2,128)S(1)} collective-permute-done((f32[2,2,64]{1,0,2:T(2,128)S(1)}, f32[2,2,64]{1,0,2:T(2,128)S(1)}, u32[]{:S(2)}, u32[]{:S(2)}) %collective-permute-start) | collective-permute-done | bytes 1056 | tf_op jit(solution)/shard_map/while/body/eval_jaxpr/ppermute | solution.py:28
  387.7 7.7 %collective-permute-done = f32[2,2,64]{1,0,2:T(2,128)S(1)} collective-permute-done((f32[2,2,64]{1,0,2:T(2,128)S(1)}, f32[2,2,64]{1,0,2:T(2,128)S(1)}, u32[]{:S(2)}, u32[]{:S(2)}) %collective-permute-start) | collective-permute-done | bytes 1056 | tf_op jit(solution)/shard_map/while/body/eval_jaxpr/ppermute | solution.py:28
  396.7 7.7 %collective-permute-done = f32[2,2,64]{1,0,2:T(2,128)S(1)} collective-permute-done((f32[2,2,64]{1,0,2:T(2,128)S(1)}, f32[2,2,64]{1,0,2:T(2,128)S(1)}, u32[]{:S(2)}, u32[]{:S(2)}) %collective-permute-start) | collective-permute-done | bytes 1056 | tf_op jit(solution)/shard_map/while/body/eval_jaxpr/ppermute | solution.py:28
  405.6 7.8 %collective-permute-done = f32[2,2,64]{1,0,2:T(2,128)S(1)} collective-permute-done((f32[2,2,64]{1,0,2:T(2,128)S(1)}, f32[2,2,64]{1,0,2:T(2,128)S(1)}, u32[]{:S(2)}, u32[]{:S(2)}) %collective-permute-start) | collective-permute-done | bytes 1056 | tf_op jit(solution)/shard_map/while/body/eval_jaxpr/ppermute | solution.py:28
  414.7 7.8 %collective-permute-done = f32[2,2,64]{1,0,2:T(2,128)S(1)} collective-permute-done((f32[2,2,64]{1,0,2:T(2,128)S(1)}, f32[2,2,64]{1,0,2:T(2,128)S(1)}, u32[]{:S(2)}, u32[]{:S(2)}) %collective-permute-start) | collective-permute-done | bytes 1056 | tf_op jit(solution)/shard_map/while/body/eval_jaxpr/ppermute | solution.py:28
  423.7 7.7 %collective-permute-done = f32[2,2,64]{1,0,2:T(2,128)S(1)} collective-permute-done((f32[2,2,64]{1,0,2:T(2,128)S(1)}, f32[2,2,64]{1,0,2:T(2,128)S(1)}, u32[]{:S(2)}, u32[]{:S(2)}) %collective-permute-start) | collective-permute-done | bytes 1056 | tf_op jit(solution)/shard_map/while/body/eval_jaxpr/ppermute | solution.py:28
  432.6 7.7 %collective-permute-done = f32[2,2,64]{1,0,2:T(2,128)S(1)} collective-permute-done((f32[2,2,64]{1,0,2:T(2,128)S(1)}, f32[2,2,64]{1,0,2:T(2,128)S(1)}, u32[]{:S(2)}, u32[]{:S(2)}) %collective-permute-start) | collective-permute-done | bytes 1056 | tf_op jit(solution)/shard_map/while/body/eval_jaxpr/ppermute | solution.py:28
  441.6 7.7 %collective-permute-done = f32[2,2,64]{1,0,2:T(2,128)S(1)} collective-permute-done((f32[2,2,64]{1,0,2:T(2,128)S(1)}, f32[2,2,64]{1,0,2:T(2,128)S(1)}, u32[]{:S(2)}, u32[]{:S(2)}) %collective-permute-start) | collective-permute-done | bytes 1056 | tf_op jit(solution)/shard_map/while/body/eval_jaxpr/ppermute | solution.py:28
  450.5 7.7 %collective-permute-done = f32[2,2,64]{1,0,2:T(2,128)S(1)} collective-permute-done((f32[2,2,64]{1,0,2:T(2,128)S(1)}, f32[2,2,64]{1,0,2:T(2,128)S(1)}, u32[]{:S(2)}, u32[]{:S(2)}) %collective-permute-start) | collective-permute-done | bytes 1056 | tf_op jit(solution)/shard_map/while/body/eval_jaxpr/ppermute | solution.py:28
  (373 shorter events, 140.5 us)
Async XLA Ops:
  0.6 320.7 %copy-start = (bf16[256,512]{1,0:T(8,128)(2,1)S(1)}, bf16[256,512]{1,0:T(8,128)(2,1)}, u32[]{:S(2)}) copy-start(bf16[256,512]{1,0:T(8,128)(2,1)} %param.23) | copy-start | bytes 786436
  7.5 18.1 %collective-permute-start.4 = (bf16[512,256]{1,0:T(8,128)(2,1)}, bf16[512,256]{1,0:T(8,128)(2,1)S(1)}, u32[]{:S(2)}, u32[]{:S(2)}) collective-permute-start(bf16[512,256]{1,0:T(8,128)(2,1)} %get-tuple-element.270), channel_id=1, source_target_pairs={{1,0},{2,1},{3,2},{4,3},{5,4},{6,5},{7,6},{8,7},{9,8},{10,9},{11,1... | collective-permute-start | bytes 786440 | tf_op jit(solution)/shard_map/ppermute | solution.py:18
  8.9 16.7 %collective-permute-start.3 = (bf16[512,256]{1,0:T(8,128)(2,1)S(1)}, bf16[512,256]{1,0:T(8,128)(2,1)S(1)}, u32[]{:S(2)}, u32[]{:S(2)}) collective-permute-start(bf16[512,256]{1,0:T(8,128)(2,1)S(1)} %get-tuple-element.271), channel_id=1, source_target_pairs={{0,1},{1,2},{2,3},{3,4},{4,5},{5,6},{6,7},{7,8},{8,9},{9,10},{10,1... | collective-permute-start | bytes 786440 | tf_op jit(solution)/shard_map/ppermute | solution.py:16
  12.1 13.6 %copy-start.46 = (bf16[128]{0:T(256)(128)(2,1)S(1)}, bf16[128]{0:T(256)(128)(2,1)}, u32[]{:S(2)}) copy-start(bf16[128]{0:T(256)(128)(2,1)} %param.22) | copy-start | bytes 772
  13.2 17.8 %collective-permute-start.1 = (f32[512,6]{1,0:T(8,128)}, f32[512,6]{1,0:T(8,128)S(1)}, u32[]{:S(2)}, u32[]{:S(2)}) collective-permute-start(f32[512,6]{1,0:T(8,128)} %get-tuple-element.268), channel_id=1, source_target_pairs={{0,1},{1,2},{2,3},{3,4},{4,5},{5,6},{6,7},{7,8},{8,9},{9,10},{10,1... | collective-permute-start | bytes 36872 | tf_op jit(solution)/shard_map/ppermute | solution.py:16
  13.2 18.5 %collective-permute-start.2 = (f32[512,6]{1,0:T(8,128)}, f32[512,6]{1,0:T(8,128)}, u32[]{:S(2)}, u32[]{:S(2)}) collective-permute-start(f32[512,6]{1,0:T(8,128)} %get-tuple-element.269), channel_id=1, source_target_pairs={{1,0},{2,1},{3,2},{4,3},{5,4},{6,5},{7,6},{8,7},{9,8},{10,9},{11,1... | collective-permute-start | bytes 36872 | tf_op jit(solution)/shard_map/ppermute | solution.py:18
  17.1 19.3 %copy-start.39 = (pred[1024]{0:T(1024)(128)(4,1)}, pred[1024]{0:T(1024)(128)(4,1)S(1)}, u32[]{:S(2)}) copy-start(pred[1024]{0:T(1024)(128)(4,1)S(1)} %compare_and_fusion.7) | copy-start | bytes 3076
  17.1 16.3 %copy-start.15 = (s32[1024]{0:T(1024)}, s32[1024]{0:T(1024)S(1)}, u32[]{:S(2)}) copy-start(s32[1024]{0:T(1024)S(1)} %get-tuple-element.316) | copy-start | bytes 12292
  17.1 19.9 %copy-start.13 = (s32[1024]{0:T(1024)}, s32[1024]{0:T(1024)S(1)}, u32[]{:S(2)}) copy-start(s32[1024]{0:T(1024)S(1)} %get-tuple-element.317) | copy-start | bytes 12292
  72.1 55.1 %copy-start.12 = (f32[32,32]{1,0:T(8,128)S(1)}, f32[32,32]{1,0:T(8,128)}, u32[]{:S(2)}) copy-start(f32[32,32]{1,0:T(8,128)} %cosine_multiply_fusion) | copy-start | bytes 12292
  72.2 55.9 %copy-start.44 = (f32[2]{0:T(128)S(1)}, f32[2]{0:T(128)}, u32[]{:S(2)}) copy-start(f32[2]{0:T(128)} %get-tuple-element.314) | copy-start | bytes 28
  72.2 55.9 %copy-start.45 = (f32[2]{0:T(128)S(1)}, f32[2]{0:T(128)}, u32[]{:S(2)}) copy-start(f32[2]{0:T(128)} %get-tuple-element.315) | copy-start | bytes 28
  74.1 95.6 %copy-start.47 = (s32[3,64]{1,0:T(4,128)S(1)}, s32[3,64]{1,0:T(4,128)}, u32[]{:S(2)}) copy-start(s32[3,64]{1,0:T(4,128)} %param.26) | copy-start | bytes 2308
  74.1 95.6 %copy-start.52 = (f32[3]{0:T(128)S(1)}, f32[3]{0:T(128)}, u32[]{:S(2)}) copy-start(f32[3]{0:T(128)} %constant.228) | copy-start | bytes 40
  77.7 149.9 %copy-start.5 = (bf16[512,256]{1,0:T(8,128)(2,1)S(1)}, bf16[512,256]{1,0:T(8,128)(2,1)}, u32[]{:S(2)}) copy-start(bf16[512,256]{1,0:T(8,128)(2,1)} %copy-done.4) | copy-start | bytes 786436
  127.2 100.5 %copy-start.3 = (bf16[512,256]{1,0:T(8,128)(2,1)S(1)}, bf16[512,256]{1,0:T(8,128)(2,1)}, u32[]{:S(2)}) copy-start(bf16[512,256]{1,0:T(8,128)(2,1)} %copy-done.2) | copy-start | bytes 786436
  127.2 100.5 %copy-start.16 = (s32[1024]{0:T(1024)S(1)}, s32[1024]{0:T(1024)}, u32[]{:S(2)}) copy-start(s32[1024]{0:T(1024)} %copy-done.15) | copy-start | bytes 12292
  324.7 7.9 %collective-permute-start = (f32[2,2,64]{1,0,2:T(2,128)S(1)}, f32[2,2,64]{1,0,2:T(2,128)S(1)}, u32[]{:S(2)}, u32[]{:S(2)}) collective-permute-start(f32[2,2,64]{1,0,2:T(2,128)S(1)} %get-tuple-element.379), channel_id=1, source_target_pairs={{240,0},{0,16},{16,32},{32,48},{48,64},{64,80},{80,96},{96,112},{1... | collective-permute-start | bytes 3080 | tf_op jit(solution)/shard_map/while/body/eval_jaxpr/ppermute | solution.py:28
  333.6 8.0 %collective-permute-start = (f32[2,2,64]{1,0,2:T(2,128)S(1)}, f32[2,2,64]{1,0,2:T(2,128)S(1)}, u32[]{:S(2)}, u32[]{:S(2)}) collective-permute-start(f32[2,2,64]{1,0,2:T(2,128)S(1)} %get-tuple-element.379), channel_id=1, source_target_pairs={{240,0},{0,16},{16,32},{32,48},{48,64},{64,80},{80,96},{96,112},{1... | collective-permute-start | bytes 3080 | tf_op jit(solution)/shard_map/while/body/eval_jaxpr/ppermute | solution.py:28
  342.5 8.1 %collective-permute-start = (f32[2,2,64]{1,0,2:T(2,128)S(1)}, f32[2,2,64]{1,0,2:T(2,128)S(1)}, u32[]{:S(2)}, u32[]{:S(2)}) collective-permute-start(f32[2,2,64]{1,0,2:T(2,128)S(1)} %get-tuple-element.379), channel_id=1, source_target_pairs={{240,0},{0,16},{16,32},{32,48},{48,64},{64,80},{80,96},{96,112},{1... | collective-permute-start | bytes 3080 | tf_op jit(solution)/shard_map/while/body/eval_jaxpr/ppermute | solution.py:28
  351.6 8.0 %collective-permute-start = (f32[2,2,64]{1,0,2:T(2,128)S(1)}, f32[2,2,64]{1,0,2:T(2,128)S(1)}, u32[]{:S(2)}, u32[]{:S(2)}) collective-permute-start(f32[2,2,64]{1,0,2:T(2,128)S(1)} %get-tuple-element.379), channel_id=1, source_target_pairs={{240,0},{0,16},{16,32},{32,48},{48,64},{64,80},{80,96},{96,112},{1... | collective-permute-start | bytes 3080 | tf_op jit(solution)/shard_map/while/body/eval_jaxpr/ppermute | solution.py:28
  360.6 8.0 %collective-permute-start = (f32[2,2,64]{1,0,2:T(2,128)S(1)}, f32[2,2,64]{1,0,2:T(2,128)S(1)}, u32[]{:S(2)}, u32[]{:S(2)}) collective-permute-start(f32[2,2,64]{1,0,2:T(2,128)S(1)} %get-tuple-element.379), channel_id=1, source_target_pairs={{240,0},{0,16},{16,32},{32,48},{48,64},{64,80},{80,96},{96,112},{1... | collective-permute-start | bytes 3080 | tf_op jit(solution)/shard_map/while/body/eval_jaxpr/ppermute | solution.py:28
  369.6 8.0 %collective-permute-start = (f32[2,2,64]{1,0,2:T(2,128)S(1)}, f32[2,2,64]{1,0,2:T(2,128)S(1)}, u32[]{:S(2)}, u32[]{:S(2)}) collective-permute-start(f32[2,2,64]{1,0,2:T(2,128)S(1)} %get-tuple-element.379), channel_id=1, source_target_pairs={{240,0},{0,16},{16,32},{32,48},{48,64},{64,80},{80,96},{96,112},{1... | collective-permute-start | bytes 3080 | tf_op jit(solution)/shard_map/while/body/eval_jaxpr/ppermute | solution.py:28
  378.5 8.0 %collective-permute-start = (f32[2,2,64]{1,0,2:T(2,128)S(1)}, f32[2,2,64]{1,0,2:T(2,128)S(1)}, u32[]{:S(2)}, u32[]{:S(2)}) collective-permute-start(f32[2,2,64]{1,0,2:T(2,128)S(1)} %get-tuple-element.379), channel_id=1, source_target_pairs={{240,0},{0,16},{16,32},{32,48},{48,64},{64,80},{80,96},{96,112},{1... | collective-permute-start | bytes 3080 | tf_op jit(solution)/shard_map/while/body/eval_jaxpr/ppermute | solution.py:28
  387.4 8.0 %collective-permute-start = (f32[2,2,64]{1,0,2:T(2,128)S(1)}, f32[2,2,64]{1,0,2:T(2,128)S(1)}, u32[]{:S(2)}, u32[]{:S(2)}) collective-permute-start(f32[2,2,64]{1,0,2:T(2,128)S(1)} %get-tuple-element.379), channel_id=1, source_target_pairs={{240,0},{0,16},{16,32},{32,48},{48,64},{64,80},{80,96},{96,112},{1... | collective-permute-start | bytes 3080 | tf_op jit(solution)/shard_map/while/body/eval_jaxpr/ppermute | solution.py:28
  396.4 8.0 %collective-permute-start = (f32[2,2,64]{1,0,2:T(2,128)S(1)}, f32[2,2,64]{1,0,2:T(2,128)S(1)}, u32[]{:S(2)}, u32[]{:S(2)}) collective-permute-start(f32[2,2,64]{1,0,2:T(2,128)S(1)} %get-tuple-element.379), channel_id=1, source_target_pairs={{240,0},{0,16},{16,32},{32,48},{48,64},{64,80},{80,96},{96,112},{1... | collective-permute-start | bytes 3080 | tf_op jit(solution)/shard_map/while/body/eval_jaxpr/ppermute | solution.py:28
  405.3 8.1 %collective-permute-start = (f32[2,2,64]{1,0,2:T(2,128)S(1)}, f32[2,2,64]{1,0,2:T(2,128)S(1)}, u32[]{:S(2)}, u32[]{:S(2)}) collective-permute-start(f32[2,2,64]{1,0,2:T(2,128)S(1)} %get-tuple-element.379), channel_id=1, source_target_pairs={{240,0},{0,16},{16,32},{32,48},{48,64},{64,80},{80,96},{96,112},{1... | collective-permute-start | bytes 3080 | tf_op jit(solution)/shard_map/while/body/eval_jaxpr/ppermute | solution.py:28
  414.4 8.1 %collective-permute-start = (f32[2,2,64]{1,0,2:T(2,128)S(1)}, f32[2,2,64]{1,0,2:T(2,128)S(1)}, u32[]{:S(2)}, u32[]{:S(2)}) collective-permute-start(f32[2,2,64]{1,0,2:T(2,128)S(1)} %get-tuple-element.379), channel_id=1, source_target_pairs={{240,0},{0,16},{16,32},{32,48},{48,64},{64,80},{80,96},{96,112},{1... | collective-permute-start | bytes 3080 | tf_op jit(solution)/shard_map/while/body/eval_jaxpr/ppermute | solution.py:28
  423.4 8.0 %collective-permute-start = (f32[2,2,64]{1,0,2:T(2,128)S(1)}, f32[2,2,64]{1,0,2:T(2,128)S(1)}, u32[]{:S(2)}, u32[]{:S(2)}) collective-permute-start(f32[2,2,64]{1,0,2:T(2,128)S(1)} %get-tuple-element.379), channel_id=1, source_target_pairs={{240,0},{0,16},{16,32},{32,48},{48,64},{64,80},{80,96},{96,112},{1... | collective-permute-start | bytes 3080 | tf_op jit(solution)/shard_map/while/body/eval_jaxpr/ppermute | solution.py:28
  432.3 8.0 %collective-permute-start = (f32[2,2,64]{1,0,2:T(2,128)S(1)}, f32[2,2,64]{1,0,2:T(2,128)S(1)}, u32[]{:S(2)}, u32[]{:S(2)}) collective-permute-start(f32[2,2,64]{1,0,2:T(2,128)S(1)} %get-tuple-element.379), channel_id=1, source_target_pairs={{240,0},{0,16},{16,32},{32,48},{48,64},{64,80},{80,96},{96,112},{1... | collective-permute-start | bytes 3080 | tf_op jit(solution)/shard_map/while/body/eval_jaxpr/ppermute | solution.py:28
  441.3 8.0 %collective-permute-start = (f32[2,2,64]{1,0,2:T(2,128)S(1)}, f32[2,2,64]{1,0,2:T(2,128)S(1)}, u32[]{:S(2)}, u32[]{:S(2)}) collective-permute-start(f32[2,2,64]{1,0,2:T(2,128)S(1)} %get-tuple-element.379), channel_id=1, source_target_pairs={{240,0},{0,16},{16,32},{32,48},{48,64},{64,80},{80,96},{96,112},{1... | collective-permute-start | bytes 3080 | tf_op jit(solution)/shard_map/while/body/eval_jaxpr/ppermute | solution.py:28
  450.2 8.0 %collective-permute-start = (f32[2,2,64]{1,0,2:T(2,128)S(1)}, f32[2,2,64]{1,0,2:T(2,128)S(1)}, u32[]{:S(2)}, u32[]{:S(2)}) collective-permute-start(f32[2,2,64]{1,0,2:T(2,128)S(1)} %get-tuple-element.379), channel_id=1, source_target_pairs={{240,0},{0,16},{16,32},{32,48},{48,64},{64,80},{80,96},{96,112},{1... | collective-permute-start | bytes 3080 | tf_op jit(solution)/shard_map/while/body/eval_jaxpr/ppermute | solution.py:28
  (40 other events, 179.7 us)
where the time goes:
time: 462 us; the launch traced here: 460 us
  blocking collectives  144 us (31%)
  local copies, waits for them, and re-layouts  125 us (27%)
  waiting for transfers between devices  114 us (25%)
  other arithmetic  41.6 us (9%)
  matrix products  24.6 us (5%)
  starting transfers between devices  7.66 us (2%)
    ppermute x15, waiting for transfers between devices, from_behind(): return lax.ppermute(block, axis, route)  114 us
    psum x1, blocking collectives, on_device(): sfac = lax.psum(partial_sums, 'space')  53.1 us
    all_gather x1, blocking collectives, on_device(): piece = lax.all_gather(stacked, 'bead', axis=0, tiled=True)  49.5 us
    all_gather x1, blocking collectives, on_device(): piece = lax.all_gather(rotated, 'bead', axis=0, tiled=True)  41 us
    gather x8, local copies, waits for them, and re-layouts, on_device(): rows = jnp.take(extended, idx, axis=0).reshape(atoms_dev, per_dev, width)  37.7 us
    convert_element_type x16, local copies, waits for them, and re-layouts, on_device(): agg = agg + weight[:, :, None] * rows.astype(jnp.float32)  34.1 us
    gather x16, local copies, waits for them, and re-layouts, on_device(): picked = jnp.take(small_table, idx, axis=0)  29.8 us
    convert_element_type x8, other arithmetic, on_device(): agg = agg + weight[:, :, None] * rows.astype(jnp.float32)  13.8 us
  transfers between devices with their start and end apart: 19, of which 15 were waited for; matrix products, arithmetic and copies ran while one was open for 4% of the time, Pallas kernels for 0%

commit v1 on v0

v1 whole, which is shorter than its diff:
```python
import functools
import math

import jax
import jax.numpy as jnp
import numpy as np
from jax import lax
from jax.experimental import pallas as pl
from jax.experimental.pallas import tpu as pltpu
from jax.sharding import PartitionSpec as P

MESH = pl.DeviceIdType.MESH
F32 = jnp.float32
BF16 = jnp.bfloat16
HIGHEST = lax.Precision.HIGHEST
N = 16
APD = 1024
GHOST = 512
EXT = 2048
W = 128
SLOTS = 8
TILE = 256
BOX = 32.0


def dct_matrix(order):
    k = np.arange(order)[:, None]
    b = np.arange(order)[None, :]
    scale = np.where(k == 0, np.sqrt(1.0 / order), np.sqrt(2.0 / order))
    return scale * np.cos(math.pi * k * (b + 0.5) / order)


def mode_tables():
    c = dct_matrix(32)
    forward = np.zeros((224, 256), np.float32)
    backward = np.zeros((96, 96), np.float32)
    ids = np.arange(N)
    for h in range(2):
        for kind in range(2):
            for comp in range(3):
                rows = 96 * h + 48 * kind + 16 * comp + ids
                for half in range(2):
                    par = h if half == 0 else 1 - h
                    cols = 128 * half + 8 * ids + 3 * kind + comp
                    forward[np.ix_(rows, cols)] = c[np.ix_(2 * ids + h, 2 * ids + par)]
        for comp in range(3):
            rows = 48 * h + 16 * comp + ids
            for half in range(2):
                par = h if half == 0 else 1 - h
                cols = 48 * half + 16 * comp + ids
                backward[np.ix_(rows, cols)] = c[np.ix_(2 * ids + par, 2 * ids + h)].T
    forward[192 + ids, 8 * ids + 6] = 1.0
    forward[208 + ids, 8 * ids + 7] = 1.0
    return forward, backward


def other(axis, offset):
    return {axis: lax.rem(lax.axis_index(axis) + offset, N)}


def lane_gather(row, index):
    return jnp.take_along_axis(row, index, axis=1, mode="promise_in_bounds")


def cos_turns(t):
    t = t - jnp.round(t)
    s = t * t
    u = s * (4.0 * math.pi * math.pi / 16.0)
    c = 1.0 + u * (-0.5 + u * (1.0 / 24 + u * (-1.0 / 720 + u * (1.0 / 40320 - u / 3628800))))
    m = c - 1.0
    m = 2.0 * m * (m + 2.0)
    m = 2.0 * m * (m + 2.0)
    return 1.0 + m


def kernel(
    feats,
    pos,
    send,
    nbr,
    mask,
    w_pair,
    w_in,
    w_out,
    omega,
    q_index,
    forward,
    backward,
    new_feats,
    new_pos,
    corr,
    table,
    small_out,
    ghost_out,
    ghost_in,
    coeff,
    columns,
    dense,
    beadrow,
    mode_out,
    mode_in,
    back_out,
    back_in,
    sum_out,
    sum_in,
    all_in,
    small_send,
    small_recv,
    ghost_send,
    ghost_recv,
    mode_send,
    mode_recv,
    back_send,
    back_recv,
    sum_send,
    sum_recv,
    all_send,
    all_recv,
):
    bead = lax.axis_index("bead")
    space = lax.axis_index("space")
    barrier = pltpu.get_barrier_semaphore()
    for axis in ("bead", "space"):
        for o in range(1, N):
            pl.semaphore_signal(barrier, inc=1, device_id=other(axis, o), device_id_type=MESH)

    lane = lax.broadcasted_iota(jnp.int32, (8, 128), 1)
    low_half = lane < 64

    pair_rows = jnp.broadcast_to(w_pair[...], (16, W))
    for b in range(2):
        strength = lax.dot_general(
            pair_rows, feats[b], (((1,), (1,)), ((), ())), preferred_element_type=F32
        )
        table[4 * b : 4 * b + 3, 0:APD] = pos[b]
        table[4 * b + 3 : 4 * b + 4, 0:APD] = strength[0:1]
        beadrow[b, 0:3] = pos[b]
        om = jnp.full((1, APD), omega[b], F32)
        beadrow[b, 6:7] = jnp.cos(om)
        beadrow[b, 7:8] = jnp.sin(om)

    for side in range(2):
        for blk in range(4):
            idx = jnp.broadcast_to(send[0, side : side + 1, 128 * blk : 128 * blk + 128], (8, 128))
            hi = lax.shift_right_logical(idx, 7)
            lo = lax.bitwise_and(idx, 127)
            acc = jnp.zeros((8, 128), F32)
            for h in range(8):
                got = lane_gather(table[:, 128 * h : 128 * h + 128], lo)
                acc = jnp.where(hi == h, got, acc)
            small_out[side, :, 128 * blk : 128 * blk + 128] = acc

    pl.semaphore_wait(barrier, 2 * (N - 1))

    small = []
    for side, step in ((0, N - 1), (1, 1)):
        start = APD + GHOST if side == 0 else APD
        copy = pltpu.make_async_remote_copy(
            src_ref=small_out.at[side],
            dst_ref=table.at[:, pl.ds(start, GHOST)],
            send_sem=small_send.at[side],
            recv_sem=small_recv.at[side],
            device_id=other("space", step),
            device_id_type=MESH,
        )
        copy.start()
        small.append(copy)

    both = jnp.concatenate([feats[0], feats[1]], axis=1)
    wide = lax.broadcasted_iota(jnp.int32, (128, APD), 1)
    ghosts = []
    for side, step in ((0, N - 1), (1, 1)):
        for blk in range(4):
            idx = jnp.broadcast_to(
                send[0, side : side + 1, 128 * blk : 128 * blk + 128], (128, 128)
            )
            col = jnp.transpose(idx)[:, 0:1]
            hot = (col == wide).astype(F32).astype(BF16)
            rows = jnp.dot(hot, both, preferred_element_type=F32).astype(BF16)
            ghost_out[side, 0, 128 * blk : 128 * blk + 128] = rows[:, 0:W]
            ghost_out[side, 1, 128 * blk : 128 * blk + 128] = rows[:, W:]
        copy = pltpu.make_async_remote_copy(
            src_ref=ghost_out.at[side],
            dst_ref=ghost_in.at[1 - side],
            send_sem=ghost_send.at[side],
            recv_sem=ghost_recv.at[side],
            device_id=other("space", step),
            device_id_type=MESH,
        )
        copy.start()
        ghosts.append(copy)

    for copy in small:
        copy.wait_recv()

    def block(blk, _):
        at = pl.ds(pl.multiple_of(blk * 128, 128), 128)
        idx = nbr[:, at]
        live = mask[:, at].astype(F32)
        hi = lax.shift_right_logical(idx, 7)
        lo = lax.bitwise_and(idx, 127)
        picked = [jnp.zeros((8, 128), F32) for _ in range(8)]
        for h in range(EXT // 128):
            hit = hi == h
            for q in range(8):
                row = jnp.broadcast_to(table[q : q + 1, 128 * h : 128 * h + 128], (8, 128))
                picked[q] = jnp.where(hit, lane_gather(row, lo), picked[q])
        code = (128 + lo).astype(F32) * lax.shift_left(jnp.ones_like(hi), hi).astype(F32)
        cs = []
        for b in range(2):
            d = []
            for c in range(3):
                d.append(table[4 * b + c : 4 * b + c + 1, at] - picked[4 * b + c])
            first = d[0]
            first = jnp.where(
                first > BOX / 2,
                first - BOX,
                jnp.where(first < -BOX / 2, first + BOX, first),
            )
            d[0] = first
            dist = d[0] * d[0] + d[1] * d[1] + d[2] * d[2]
            weight = live / (1.0 + dist / 4.0)
            pair = weight * (table[4 * b + 3 : 4 * b + 4, at] + picked[4 * b + 3])
            for c in range(3):
                beadrow[b, 3 + c : 4 + c, at] = jnp.sum(pair * d[c], axis=0, keepdims=True)
            cs.append(weight)
        total = list(cs)
        for r in range(1, SLOTS):
            same = pltpu.roll(idx, r, 0) == idx
            for b in range(2):
                total[b] = total[b] + jnp.where(same, pltpu.roll(cs[b], r, 0), 0.0)
        stack = jnp.concatenate(
            [code, total[0], total[1], jnp.zeros((104, 128), F32)], axis=0
        )
        columns[at, :] = jnp.transpose(stack)
        one = beadrow[0, :, at]
        two = beadrow[1, :, at]
        mode_out[2 * blk] = jnp.where(low_half, one, pltpu.roll(two, 64, 1))
        mode_out[2 * blk + 1] = jnp.where(low_half, pltpu.roll(one, 64, 1), two)
        return 0

    lax.fori_loop(0, APD // 128, block, 0)

    def exchange(axis, source, target, send_sem, recv_sem):
        me = lax.axis_index(axis)
        copies = []
        for o in range(1, N):
            to = lax.rem(me + o, N)
            copy = pltpu.make_async_remote_copy(
                src_ref=source(to),
                dst_ref=target(me, N - o),
                send_sem=send_sem.at[o],
                recv_sem=recv_sem.at[N - o],
                device_id={axis: to},
                device_id_type=MESH,
            )
            copy.start()
            copies.append(copy)
        return copies

    mode_copies = exchange(
        "bead", lambda to: mode_out.at[to], lambda me, r: mode_in.at[me], mode_send, mode_recv
    )
    mode_in[bead] = mode_out[bead]
    for copy in ghosts:
        copy.wait_recv()

    lane_code = (128 + lax.broadcasted_iota(jnp.int32, (16, 128), 1)).astype(F32)

    def dense_tile(t):
        def strip(s, _):
            at = pl.ds(pl.multiple_of(t * TILE + s * 16, 16), 16)
            cols = columns[at, :]

            def spread(j):
                return jnp.broadcast_to(cols[:, j : j + 1], (16, 128)).astype(BF16)

            codes = [spread(k) for k in range(SLOTS)]
            c0 = [spread(8 + k) for k in range(SLOTS)]
            c1 = [spread(16 + k) for k in range(SLOTS)]
            row = pl.ds(pl.multiple_of(s * 16, 16), 16)
            for h in range(EXT // 128):
                here = (lane_code * float(2**h)).astype(BF16)
                a0 = jnp.zeros((16, 128), BF16)
                a1 = jnp.zeros((16, 128), BF16)
                for k in range(SLOTS):
                    hit = codes[k] == here
                    a0 = jnp.where(hit, c0[k], a0)
                    a1 = jnp.where(hit, c1[k], a1)
                dense[0, row, 128 * h : 128 * h + 128] = a0
                dense[1, row, 128 * h : 128 * h + 128] = a1
            return 0

        lax.fori_loop(0, TILE // 16, strip, 0)
        at = pl.ds(pl.multiple_of(t * TILE, TILE), TILE)
        for b in range(2):
            agg = jnp.dot(dense[b, :, 0:APD], feats[b], preferred_element_type=F32)
            agg += jnp.dot(
                dense[b, :, APD : APD + GHOST], ghost_in[0, b], preferred_element_type=F32
            )
            agg += jnp.dot(dense[b, :, APD + GHOST :], ghost_in[1, b], preferred_element_type=F32)
            mine = feats[b, at, :]
            joined = jnp.concatenate([mine, agg.astype(BF16)], axis=1)
            x = jnp.dot(joined, w_in[...], preferred_element_type=F32)
            hidden = (x * (0.5 * (1.0 + jnp.tanh(0.5 * x)))).astype(BF16)
            out = mine.astype(F32) + jnp.dot(hidden, w_out[...], preferred_element_type=F32)
            new_feats[b, at, :] = out.astype(BF16)

    def dense_tiles(first, last):
        def step(t, _):
            dense_tile(t)
            return 0

        lax.fori_loop(first, last, step, 0)

    dense_tiles(0, 1)

    for copy in mode_copies:
        copy.wait_recv()
    low = lax.broadcasted_iota(jnp.int32, (48, 128), 1) < 64
    z = mode_in[...].reshape(128, 128)
    z = jnp.concatenate([z, pltpu.roll(z, 64, 1)], axis=0)
    y = jnp.dot(forward[...], z, precision=HIGHEST, preferred_element_type=F32)
    cosw = jnp.concatenate([y[192:208]] * 3, axis=0)
    sinw = jnp.concatenate([y[208:224]] * 3, axis=0)
    rotated = cosw * jnp.where(low, y[0:48], y[96:144]) + sinw * jnp.where(
        low, y[48:96], y[144:192]
    )
    z = jnp.concatenate([rotated, pltpu.roll(rotated, 64, 1)], axis=0)
    y = jnp.dot(backward[...], z, precision=HIGHEST, preferred_element_type=F32)
    moved = jnp.where(low, y[0:48], y[48:96])
    for d in range(N):
        for c in range(3):
            back_out[d, c : c + 1] = moved[16 * c + d : 16 * c + d + 1]
    back_copies = exchange(
        "bead", lambda to: back_out.at[to], lambda me, r: back_in.at[me], back_send, back_recv
    )
    back_in[bead] = back_out[bead]

    dense_tiles(1, 2)

    q0 = q_index[0:1, :]
    pick = 4 * (q_index[1:2, :] - 1) + (q_index[2:3, :] - 1)
    pick = jnp.concatenate([pick, pick + 16], axis=1)
    q0 = jnp.concatenate([q0, q0], axis=1)
    row64 = lax.broadcasted_iota(jnp.int32, (64, 128), 0)
    choose = (lax.bitwise_and(row64, 31) == pick).astype(F32)
    row16 = lax.broadcasted_iota(jnp.int32, (16, 128), 0)
    row8 = lax.bitwise_and(row16, 7)
    lane16 = lax.broadcasted_iota(jnp.int32, (16, 128), 1)
    direct = (row8 == q0 - 1).astype(F32)
    crossed = jnp.where(row8 == q0 + 3, jnp.where(lane16 < 64, -1.0, 1.0), 0.0)

    for copy in back_copies:
        copy.wait_recv()
    for m in range(8):
        one = back_in[2 * m]
        two = back_in[2 * m + 1]
        at = slice(128 * m, 128 * m + 128)
        first = jnp.where(low_half, one, pltpu.roll(two, 64, 1))
        second = jnp.where(low_half, pltpu.roll(one, 64, 1), two)
        new_pos[0, :, at] = first[0:3]
        new_pos[1, :, at] = second[0:3]

    r8 = lax.broadcasted_iota(jnp.int32, (8, APD), 0)
    r32 = lax.broadcasted_iota(jnp.int32, (32, APD), 0)
    u_q = (lax.bitwise_and(r8, 3) + 1).astype(F32) * (1.0 / BOX)
    u_off = jnp.where(r8 >= 4, 0.25, 0.0)
    v_q1 = (lax.bitwise_and(lax.shift_right_logical(r32, 2), 3) + 1).astype(F32) * 0.25
    v_q2 = (lax.bitwise_and(r32, 3) + 1).astype(F32) * 0.25
    v_off = jnp.where(r32 >= 16, 0.25, 0.0)
    us, vs = [], []
    for b in range(2):
        us.append(cos_turns(u_q * new_pos[b, 0:1, :] - u_off))
        vs.append(cos_turns(v_q1 * new_pos[b, 1:2, :] + v_q2 * new_pos[b, 2:3, :] - v_off))
    raw = lax.dot_general(
        jnp.concatenate(us, axis=0),
        jnp.concatenate(vs, axis=0),
        (((1,), (1,)), ((), ())),
        precision=HIGHEST,
        preferred_element_type=F32,
    )
    own_row = lax.broadcasted_iota(jnp.int32, (16, 64), 0) < 8
    own_col = lax.broadcasted_iota(jnp.int32, (16, 64), 1) < 32
    raw = jnp.where(own_row == own_col, raw, 0.0)
    spread_q = jnp.dot(raw, choose, precision=HIGHEST, preferred_element_type=F32)
    parts = direct * spread_q + crossed * pltpu.roll(spread_q, 64, 1)
    sum_out[0:1] = jnp.sum(parts[0:8], axis=0, keepdims=True)
    sum_out[1:2] = jnp.sum(parts[8:16], axis=0, keepdims=True)

    sum_copies = exchange(
        "space", lambda to: sum_out, lambda me, r: sum_in.at[r], sum_send, sum_recv
    )
    dense_tiles(2, 3)
    for copy in sum_copies:
        copy.wait_recv()
    total = sum_out[...]
    for r in range(1, N):
        total = total + sum_in[r]
    all_in[0] = total
    all_copies = exchange(
        "bead", lambda to: all_in.at[0], lambda me, r: all_in.at[r], all_send, all_recv
    )
    dense_tiles(3, 4)
    for copy in all_copies:
        copy.wait_recv()
    every = jnp.concatenate([all_in[r] for r in range(N)], axis=0)
    for b in range(2):
        prod = every * (every[b : b + 1] * (1.0 / (APD * N)))
        both_q = prod + pltpu.roll(prod, 64, 1)
        if b:
            both_q = jnp.concatenate([both_q[1:], both_q[0:1]], axis=0)
        corr[b] = both_q[:, 0:64]

    for copy in small + ghosts + mode_copies + back_copies + sum_copies + all_copies:
        copy.wait_send()


def on_device(
    features, positions, send_rows, neighbours, nbr_mask, w_pair, w_in, w_out, omega, q_index
):
    forward, backward = mode_tables()
    vmem = pl.BlockSpec(memory_space=pltpu.VMEM)
    smem = pl.BlockSpec(memory_space=pltpu.SMEM)
    dma = pltpu.SemaphoreType.DMA
    return pl.pallas_call(
        kernel,
        out_shape=(
            jax.ShapeDtypeStruct((2, APD, W), BF16),
            jax.ShapeDtypeStruct((2, 3, APD), F32),
            jax.ShapeDtypeStruct((2, 32, 64), F32),
        ),
        in_specs=[vmem] * 8 + [smem] + [vmem] * 3,
        out_specs=(vmem, vmem, vmem),
        scratch_shapes=[
            pltpu.VMEM((8, EXT), F32),
            pltpu.VMEM((2, 8, GHOST), F32),
            pltpu.VMEM((2, 2, GHOST, W), BF16),
            pltpu.VMEM((2, 2, GHOST, W), BF16),
            pltpu.VMEM((8, 128), F32),
            pltpu.VMEM((APD, 128), F32),
            pltpu.VMEM((2, TILE, EXT), BF16),
            pltpu.VMEM((2, 8, APD), F32),
            pltpu.VMEM((N, 8, 128), F32),
            pltpu.VMEM((N, 8, 128), F32),
            pltpu.VMEM((N, 8, 128), F32),
            pltpu.VMEM((N, 8, 128), F32),
            pltpu.VMEM((2, 128), F32),
            pltpu.VMEM((N, 2, 128), F32),
            pltpu.VMEM((N, 2, 128), F32),
            dma((2,)),
            dma((2,)),
            dma((2,)),
            dma((2,)),
        ]
        + [dma((N,))] * 8,
        compiler_params=pltpu.CompilerParams(
            collective_id=0, has_side_effects=True, vmem_limit_bytes=48 * 2**20
        ),
    )(
        features,
        positions,
        send_rows,
        neighbours,
        nbr_mask,
        w_pair.reshape(1, W),
        w_in,
        w_out,
        omega,
        q_index,
        jnp.asarray(forward),
        jnp.asarray(backward),
    )


def solution(mesh):
    in_specs = (
        P("bead", "space", None),
        P("bead", None, "space"),
        P("space", None, None),
        P(None, "space"),
        P(None, "space"),
        P(),
        P(),
        P(),
        P("bead"),
        P(),
    )
    out_specs = (P("bead", "space", None), P("bead", None, "space"), P("bead", None, None))
    return jax.shard_map(
        on_device, mesh=mesh, in_specs=in_specs, out_specs=out_specs, check_vma=False
    )
```

time: 462 us -> 54 us (0.12)
  the two profiles are of different devices: /device:TPU:0 before, /device:TPU:1 now
where the time goes in v1:
time: 54 us; the launch traced here: 53.6 us
  Pallas kernels  44.7 us (83%)
  local copies, waits for them, and re-layouts  8.19 us (15%)
  between operations  0.74 us (1%)
    pallas_call x1, Pallas kernels, on_device(): pl.pallas_call(kernel, out_shape=(jax.ShapeDtypeStruct((2, APD, W), BF16)...  44.7 us
    unnamed x25, local copies, waits for them, and re-layouts  7.56 us

profile of v1, /device:TPU:1, one launch (start us, length us, event | category | flops | bytes accessed | tf_op | source)
XLA Modules:
  0.0 53.6 jit_solution(9470188840216952375)
XLA Ops:
  0.6 0.0 copy-start.4
  0.6 0.0 copy-start.7
  0.7 0.0 copy-start.8
  0.7 0.0 copy-start.9
  0.7 0.0 copy-start.10
  0.7 0.8 %copy.15.pos = f32[2,3,1024]{2,1,0:T(4,128)S(1)} copy(f32[2,3,1024]{2,0,1:T(2,128)} %param.13) | data formatting | bytes 49152 | tf_op args[1]
  1.5 0.0 copy-done.4
  1.5 0.0 copy-done.7
  1.5 0.0 copy-done.8
  1.5 0.0 copy-done.9
  1.5 0.0 copy-done.10
  1.5 0.0 copy-start
  1.5 1.0 %copy-done = bf16[2,1024,128]{2,1,0:T(8,128)(2,1)S(1)} copy-done((bf16[2,1024,128]{2,1,0:T(8,128)(2,1)S(1)}, bf16[2,1024,128]{2,1,0:T(8,128)(2,1)}, u32[]{:S(2)}) %copy-start) | copy-done | bytes 524312
  2.6 0.0 copy-start.1
  2.6 0.9 %copy-done.1 = bf16[256,512]{1,0:T(8,128)(2,1)S(1)} copy-done((bf16[256,512]{1,0:T(8,128)(2,1)S(1)}, bf16[256,512]{1,0:T(8,128)(2,1)}, u32[]{:S(2)}) %copy-start.1) | copy-done | bytes 262168
  3.5 0.0 copy-start.2
  3.5 0.9 %copy-done.2 = f32[224,256]{1,0:T(8,128)S(1)} copy-done((f32[224,256]{1,0:T(8,128)S(1)}, f32[224,256]{1,0:T(8,128)}, u32[]{:S(2)}) %copy-start.2) | copy-done | bytes 229400
  4.5 0.0 copy-start.3
  4.5 0.9 %copy-done.3 = bf16[512,128]{1,0:T(8,128)(2,1)S(1)} copy-done((bf16[512,128]{1,0:T(8,128)(2,1)S(1)}, bf16[512,128]{1,0:T(8,128)(2,1)}, u32[]{:S(2)}) %copy-start.3) | copy-done | bytes 131096
  5.4 0.0 copy-start.5
  5.4 0.8 %copy-done.5 = s32[8,1024]{1,0:T(8,128)S(1)} copy-done((s32[8,1024]{1,0:T(8,128)S(1)}, s32[8,1024]{1,0:T(8,128)}, u32[]{:S(2)}) %copy-start.5) | copy-done | bytes 32792
  6.1 0.0 copy-start.6
  6.1 0.8 %copy-done.6 = s32[8,1024]{1,0:T(8,128)S(1)} copy-done((s32[8,1024]{1,0:T(8,128)S(1)}, s32[8,1024]{1,0:T(8,128)}, u32[]{:S(2)}) %copy-start.6) | copy-done | bytes 32792
  6.9 44.7 %shard_map.139 = (bf16[2,1024,128]{2,1,0:T(8,128)(2,1)S(1)}, f32[2,3,1024]{2,1,0:T(4,128)S(1)}, f32[2,32,64]{2,1,0:T(8,128)S(1)}) custom-call(bf16[2,1024,128]{2,1,0:T(8,128)(2,1)S(1)} %copy-done, f32[2,3,1024]{2,1,0:T(4,128)S(1)} %copy.15.pos, s32[1,2,512]{2,1,0:T(2,128)S(1)} %copy-done.7, s32[8,1024]{1,0:T(8,128)S(1)} %copy-done.5, ...), custom_call_target="tpu_custom_call" | custom-call | tf_op jit(solution)/shard_map/pallas_call | solution.py:426
  51.6 0.6 %copy.16 = f32[2,3,1024]{2,0,1:T(2,128)} copy(f32[2,3,1024]{2,1,0:T(4,128)S(1)} %get-tuple-element.4) | data formatting | bytes 49152 | tf_op jit(solution)/shard_map/pallas_call | solution.py:426
  52.2 0.8 %copy.19 = bf16[2,1024,128]{2,1,0:T(8,128)(2,1)} copy(bf16[2,1024,128]{2,1,0:T(8,128)(2,1)S(1)} %get-tuple-element.9) | data formatting | bytes 1048576
  53.0 0.6 %copy.20 = f32[2,32,64]{2,1,0:T(8,128)} copy(f32[2,32,64]{2,1,0:T(8,128)S(1)} %get-tuple-element.11) | data formatting | bytes 32768
Async XLA Ops:
  0.6 0.8 %copy-start.4 = (f32[96,96]{1,0:T(8,128)S(1)}, f32[96,96]{1,0:T(8,128)}, u32[]{:S(2)}) copy-start(f32[96,96]{1,0:T(8,128)} %constant.5.clone.backward) | copy-start | bytes 110596
  0.6 0.8 %copy-start.7 = (s32[1,2,512]{2,1,0:T(2,128)S(1)}, s32[1,2,512]{2,1,0:T(2,128)}, u32[]{:S(2)}) copy-start(s32[1,2,512]{2,1,0:T(2,128)} %send.1) | copy-start | bytes 12292
  0.7 0.8 %copy-start.8 = (s32[3,64]{1,0:T(4,128)S(1)}, s32[3,64]{1,0:T(4,128)}, u32[]{:S(2)}) copy-start(s32[3,64]{1,0:T(4,128)} %q_index.1) | copy-start | bytes 2308
  0.7 0.8 %copy-start.9 = (bf16[128]{0:T(256)(128)(2,1)S(1)}, bf16[128]{0:T(256)(128)(2,1)}, u32[]{:S(2)}) copy-start(bf16[128]{0:T(256)(128)(2,1)} %param.17) | copy-start | bytes 772
  0.7 0.8 %copy-start.10 = (f32[2]{0:T(128)S(1)}, f32[2]{0:T(128)}, u32[]{:S(2)}) copy-start(f32[2]{0:T(128)} %omega.1) | copy-start | bytes 28
  1.5 1.0 %copy-start = (bf16[2,1024,128]{2,1,0:T(8,128)(2,1)S(1)}, bf16[2,1024,128]{2,1,0:T(8,128)(2,1)}, u32[]{:S(2)}) copy-start(bf16[2,1024,128]{2,1,0:T(8,128)(2,1)} %feats.1) | copy-start | bytes 1572868
  2.6 0.9 %copy-start.1 = (bf16[256,512]{1,0:T(8,128)(2,1)S(1)}, bf16[256,512]{1,0:T(8,128)(2,1)}, u32[]{:S(2)}) copy-start(bf16[256,512]{1,0:T(8,128)(2,1)} %w_in.1) | copy-start | bytes 786436
  3.5 0.9 %copy-start.2 = (f32[224,256]{1,0:T(8,128)S(1)}, f32[224,256]{1,0:T(8,128)}, u32[]{:S(2)}) copy-start(f32[224,256]{1,0:T(8,128)} %constant.4.clone.forward) | copy-start | bytes 688132
  4.5 0.9 %copy-start.3 = (bf16[512,128]{1,0:T(8,128)(2,1)S(1)}, bf16[512,128]{1,0:T(8,128)(2,1)}, u32[]{:S(2)}) copy-start(bf16[512,128]{1,0:T(8,128)(2,1)} %w_out.1) | copy-start | bytes 393220
  5.4 0.8 %copy-start.5 = (s32[8,1024]{1,0:T(8,128)S(1)}, s32[8,1024]{1,0:T(8,128)}, u32[]{:S(2)}) copy-start(s32[8,1024]{1,0:T(8,128)} %nbr.1) | copy-start | bytes 98308
  6.1 0.8 %copy-start.6 = (s32[8,1024]{1,0:T(8,128)S(1)}, s32[8,1024]{1,0:T(8,128)}, u32[]{:S(2)}) copy-start(s32[8,1024]{1,0:T(8,128)} %mask.1) | copy-start | bytes 98308

commit v2 on v1

v2 whole, which is shorter than its diff:
```python
import functools
import math

import jax
import jax.numpy as jnp
from jax import lax
from jax.experimental import pallas as pl
from jax.experimental.pallas import tpu as pltpu
from jax.sharding import PartitionSpec as P

MESH = pl.DeviceIdType.MESH
F32 = jnp.float32
BF16 = jnp.bfloat16
HIGHEST = lax.Precision.HIGHEST
N = 16
RING = 8
APD = 1024
GHOST = 512
EXT = 2048
W = 128
SLOTS = 8
TILE = 256
BOX = 32.0


def other(axis, offset):
    return {axis: lax.rem(lax.axis_index(axis) + offset, N)}


def lane_gather(row, index):
    return jnp.take_along_axis(row, index, axis=1, mode="promise_in_bounds")


def cos_turns(t):
    t = t - jnp.round(t)
    u = (t * t) * (math.pi * math.pi / 4.0)
    m = u * (-0.5 + u * (1.0 / 24 + u * (-1.0 / 720 + u * (1.0 / 40320 - u / 3628800))))
    m = 2.0 * m * (m + 2.0)
    m = 2.0 * m * (m + 2.0)
    return 1.0 + m


def dct_entry(k, bead):
    turns = lax.bitwise_and(k * (2 * bead + 1), 127).astype(F32) * (1.0 / 128.0)
    return jnp.where(k == 0, math.sqrt(1.0 / 32), math.sqrt(2.0 / 32)) * cos_turns(turns)


def kernel(
    feats_hbm,
    pos_hbm,
    send_hbm,
    nbr_hbm,
    mask_hbm,
    w_pair_hbm,
    w_in_hbm,
    w_out_hbm,
    omega_hbm,
    q_hbm,
    new_feats,
    new_pos,
    corr,
    feats,
    pos,
    send,
    nbr,
    mask,
    w_pair,
    w_in,
    w_out,
    omega,
    q_index,
    load_sem,
    table,
    small_out,
    ghost_out,
    ghost_in,
    columns,
    dense,
    pos_out,
    pos_in,
    force_out,
    force_in,
    waves,
    coeff,
    moved,
    moved_in,
    sum_in,
    all_in,
    small_send,
    small_recv,
    ghost_send,
    ghost_recv,
    pos_send,
    pos_recv,
    force_send,
    force_recv,
    moved_sem,
    sum_send,
    sum_recv,
    all_send,
    all_recv,
):
    bead = lax.axis_index("bead")
    space = lax.axis_index("space")
    ring = lax.div(bead, 2)
    half = lax.rem(bead, 2)
    barrier = pltpu.get_barrier_semaphore()

    def plane(side, step):
        return {
            "bead": 2 * ring + lax.rem(half + side, 2),
            "space": lax.rem(space + step, N),
        }

    for step in (1, N - 1) + tuple(range(2, N - 1)):
        pl.semaphore_signal(barrier, inc=1, device_id=plane(0, step), device_id_type=MESH)
    for step in range(N):
        pl.semaphore_signal(barrier, inc=1, device_id=plane(1, step), device_id_type=MESH)
    for step in range(1, RING):
        for side in range(2):
            to = 2 * lax.rem(ring + step, RING) + side
            pl.semaphore_signal(barrier, inc=1, device_id={"bead": to}, device_id_type=MESH)
    partners = (N - 1) + N + 2 * (RING - 1)

    loads = []
    for source, target in (
        (w_pair_hbm, w_pair),
        (feats_hbm, feats),
        (pos_hbm, pos),
        (send_hbm, send),
        (nbr_hbm, nbr),
        (mask_hbm, mask),
        (omega_hbm, omega),
        (w_in_hbm, w_in),
        (w_out_hbm, w_out),
        (q_hbm, q_index),
    ):
        copy = pltpu.make_async_copy(source, target, load_sem.at[len(loads)])
        copy.start()
        loads.append(copy)

    lane = lax.broadcasted_iota(jnp.int32, (8, 128), 1)

    for i in range(4):
        loads[i].wait()
    pair_rows = jnp.broadcast_to(w_pair[...], (16, W))
    for b in range(2):
        strength = lax.dot_general(
            pair_rows, feats[b], (((1,), (1,)), ((), ())), preferred_element_type=F32
        )
        for c in range(3):
            table[4 * b + c : 4 * b + c + 1, 0:APD] = pos[c, b : b + 1]
        table[4 * b + 3 : 4 * b + 4, 0:APD] = strength[0:1]

    for side in range(2):
        for blk in range(4):
            idx = jnp.broadcast_to(send[0, side : side + 1, 128 * blk : 128 * blk + 128], (8, 128))
            hi = lax.shift_right_logical(idx, 7)
            lo = lax.bitwise_and(idx, 127)
            acc = jnp.zeros((8, 128), F32)
            for h in range(8):
                got = lane_gather(table[:, 128 * h : 128 * h + 128], lo)
                acc = jnp.where(hi == h, got, acc)
            small_out[side, :, 128 * blk : 128 * blk + 128] = acc

    for i in range(4, 7):
        loads[i].wait()
    for part in range(2):
        for c in range(3):
            for b in range(2):
                for blk in range(4):
                    at = GHOST * part + 128 * blk
                    row = 8 * c + 4 * b + blk
                    pos_out[part, row : row + 1] = pos[c, b : b + 1, at : at + 128]
    angle = jnp.concatenate([jnp.full((1, 128), omega[b], F32) for b in range(2)], axis=0)
    wave_rows = jnp.concatenate([jnp.cos(angle), jnp.sin(angle), jnp.zeros((4, 128), F32)], axis=0)
    for part in range(2):
        pos_out[part, 24:32] = wave_rows

    pl.semaphore_wait(barrier, partners)

    def to_neighbour(source, target, send_sem, recv_sem, side):
        copy = pltpu.make_async_remote_copy(
            src_ref=source,
            dst_ref=target,
            send_sem=send_sem.at[side],
            recv_sem=recv_sem.at[side],
            device_id=other("space", N - 1 if side == 0 else 1),
            device_id_type=MESH,
        )
        copy.start()
        return copy

    small = []
    for side in range(2):
        start = APD + GHOST if side == 0 else APD
        small.append(
            to_neighbour(
                small_out.at[side], table.at[:, pl.ds(start, GHOST)], small_send, small_recv, side
            )
        )

    def to_beads(source, target, send_sem, recv_sem, offsets):
        copies = []
        for o in offsets:
            to = lax.rem(bead + o, N)
            copy = pltpu.make_async_remote_copy(
                src_ref=source.at[lax.rem(to, 2)],
                dst_ref=target.at[bead],
                send_sem=send_sem.at[o],
                recv_sem=recv_sem.at[N - o],
                device_id={"bead": to},
                device_id_type=MESH,
            )
            copy.start()
            copies.append(copy)
        return copies

    crossing = (7, 9, 5, 11, 3, 13, 1, 15)
    straight = (8, 6, 10, 4, 12, 2, 14)
    pos_copies = to_beads(pos_out, pos_in, pos_send, pos_recv, crossing + straight)
    pos_in[bead] = pos_out[half]

    both = jnp.concatenate([feats[0], feats[1]], axis=1)
    wide = lax.broadcasted_iota(jnp.int32, (128, APD), 1)
    ghosts = []
    for side in range(2):
        for blk in range(4):
            idx = jnp.broadcast_to(
                send[0, side : side + 1, 128 * blk : 128 * blk + 128], (128, 128)
            )
            col = jnp.transpose(idx)[:, 0:1]
            hot = (col == wide).astype(F32).astype(BF16)
            rows = jnp.dot(hot, both, preferred_element_type=F32).astype(BF16)
            ghost_out[side, 0, 128 * blk : 128 * blk + 128] = rows[:, 0:W]
            ghost_out[side, 1, 128 * blk : 128 * blk + 128] = rows[:, W:]
        ghosts.append(
            to_neighbour(ghost_out.at[side], ghost_in.at[1 - side], ghost_send, ghost_recv, side)
        )

    for copy in small:
        copy.wait_recv()

    def block(part, blk):
        at = pl.ds(pl.multiple_of(GHOST * part + 128 * blk, 128), 128)
        idx = nbr[:, at]
        live = mask[:, at].astype(F32)
        hi = lax.shift_right_logical(idx, 7)
        lo = lax.bitwise_and(idx, 127)
        picked = [jnp.zeros((8, 128), F32) for _ in range(8)]
        for h in range(EXT // 128):
            hit = hi == h
            for q in range(8):
                row = jnp.broadcast_to(table[q : q + 1, 128 * h : 128 * h + 128], (8, 128))
                picked[q] = jnp.where(hit, lane_gather(row, lo), picked[q])
        code = (128 + lo).astype(F32) * lax.shift_left(jnp.ones_like(hi), hi).astype(F32)
        cs = []
        for b in range(2):
            d = []
            for c in range(3):
                d.append(table[4 * b + c : 4 * b + c + 1, at] - picked[4 * b + c])
            first = d[0]
            d[0] = jnp.where(
                first > BOX / 2,
                first - BOX,
                jnp.where(first < -BOX / 2, first + BOX, first),
            )
            dist = d[0] * d[0] + d[1] * d[1] + d[2] * d[2]
            weight = live / (1.0 + dist / 4.0)
            pair = weight * (table[4 * b + 3 : 4 * b + 4, at] + picked[4 * b + 3])
            for c in range(3):
                row = pl.ds(8 * c + 4 * b + blk, 1)
                force_out[part, row, :] = jnp.sum(pair * d[c], axis=0, keepdims=True)
            cs.append(weight)
        total = list(cs)
        for r in range(1, SLOTS):
            same = pltpu.roll(idx, r, 0) == idx
            for b in range(2):
                total[b] = total[b] + jnp.where(same, pltpu.roll(cs[b], r, 0), 0.0)
        stack = jnp.concatenate([code, total[0], total[1], jnp.zeros((104, 128), F32)], axis=0)
        columns[at, :] = jnp.transpose(stack)

    def blocks(part):
        def step(blk, _):
            block(part, blk)
            return 0

        lax.fori_loop(0, 4, step, 0)

    blocks(1 - half)
    force_copies = to_beads(force_out, force_in, force_send, force_recv, crossing)
    blocks(half)
    force_copies += to_beads(force_out, force_in, force_send, force_recv, straight)
    force_in[bead] = force_out[half]

    for copy in pos_copies:
        copy.wait_recv()
    for source in range(N):
        waves[0, 2 * source : 2 * source + 2] = pos_in[source, 24:26]
        waves[1, 2 * source : 2 * source + 2] = pos_in[source, 26:28]
    k_rows = lax.broadcasted_iota(jnp.int32, (32, 128), 0)
    by_mode = []
    for e in range(4):
        entry = dct_entry(k_rows, 4 * ring + e)
        by_mode += [entry * waves[0], entry * waves[1]]
    rows = lax.broadcasted_iota(jnp.int32, (128, 32), 0)
    source_bead = 2 * lax.shift_right_logical(rows, 3) + lax.bitwise_and(
        lax.shift_right_logical(rows, 2), 1
    )
    spread = dct_entry(lax.broadcasted_iota(jnp.int32, (128, 32), 1), source_bead)
    coeff[...] = jnp.dot(
        spread,
        jnp.concatenate(by_mode, axis=1),
        precision=HIGHEST,
        preferred_element_type=F32,
    )

    def mix(kind, data, acc):
        for source in range(N):
            for c in range(3):
                value = data[source, 8 * c : 8 * c + 8]
                for e in range(4):
                    lanes = slice(128 * (2 * e + kind), 128 * (2 * e + kind) + 128)
                    acc[3 * e + c] = acc[3 * e + c] + coeff[8 * source : 8 * source + 8, lanes] * value
        return acc

    acc = mix(0, pos_in, [jnp.zeros((8, 128), F32) for _ in range(12)])

    for i in range(7, 10):
        loads[i].wait()
    for copy in ghosts:
        copy.wait_recv()

    lane_code = (128 + lax.broadcasted_iota(jnp.int32, (16, 128), 1)).astype(F32)

    def dense_tile(t):
        def strip(s, _):
            at = pl.ds(pl.multiple_of(t * TILE + s * 16, 16), 16)
            cols = columns[at, :]

            def spread_lane(j):
                return jnp.broadcast_to(cols[:, j : j + 1], (16, 128)).astype(BF16)

            codes = [spread_lane(k) for k in range(SLOTS)]
            c0 = [spread_lane(8 + k) for k in range(SLOTS)]
            c1 = [spread_lane(16 + k) for k in range(SLOTS)]
            row = pl.ds(pl.multiple_of(s * 16, 16), 16)
            for h in range(EXT // 128):
                here = (lane_code * float(2**h)).astype(BF16)
                a0 = jnp.zeros((16, 128), BF16)
                a1 = jnp.zeros((16, 128), BF16)
                for k in range(SLOTS):
                    hit = codes[k] == here
                    a0 = jnp.where(hit, c0[k], a0)
                    a1 = jnp.where(hit, c1[k], a1)
                dense[0, row, 128 * h : 128 * h + 128] = a0
                dense[1, row, 128 * h : 128 * h + 128] = a1
            return 0

        lax.fori_loop(0, TILE // 16, strip, 0)
        at = pl.ds(pl.multiple_of(t * TILE, TILE), TILE)
        for b in range(2):
            agg = jnp.dot(dense[b, :, 0:APD], feats[b], preferred_element_type=F32)
            agg += jnp.dot(
                dense[b, :, APD : APD + GHOST], ghost_in[0, b], preferred_element_type=F32
            )
            agg += jnp.dot(dense[b, :, APD + GHOST :], ghost_in[1, b], preferred_element_type=F32)
            mine = feats[b, at, :]
            joined = jnp.concatenate([mine, agg.astype(BF16)], axis=1)
            x = jnp.dot(joined, w_in[...], preferred_element_type=F32)
            hidden = (x * (0.5 * (1.0 + jnp.tanh(0.5 * x)))).astype(BF16)
            out = mine.astype(F32) + jnp.dot(hidden, w_out[...], preferred_element_type=F32)
            new_feats[b, at, :] = out.astype(BF16)

    def dense_tiles(first, last):
        def step(t, _):
            dense_tile(t)
            return 0

        lax.fori_loop(first, last, step, 0)

    dense_tiles(0, 1)

    q0 = q_index[0:1, :]
    pick = 4 * (q_index[1:2, :] - 1) + (q_index[2:3, :] - 1)
    pick = jnp.concatenate([pick, pick + 16], axis=1)
    q0 = jnp.concatenate([q0, q0], axis=1)
    row128 = lax.broadcasted_iota(jnp.int32, (128, 128), 0)
    choose = (lax.bitwise_and(row128, 31) == pick).astype(F32)
    row32 = lax.broadcasted_iota(jnp.int32, (32, 128), 0)
    lane32 = lax.broadcasted_iota(jnp.int32, (32, 128), 1)
    row8 = lax.bitwise_and(row32, 7)
    direct = (row8 == q0 - 1).astype(F32)
    crossed = jnp.where(row8 == q0 + 3, jnp.where(lane32 < 64, -1.0, 1.0), 0.0)
    same_bead = lax.shift_right_logical(row32, 3) == lax.shift_right_logical(lane32, 5)
    r8 = lax.broadcasted_iota(jnp.int32, (8, 128), 0)
    u_q = (lax.bitwise_and(r8, 3) + 1).astype(F32) * (1.0 / BOX)
    u_off = jnp.where(r8 >= 4, 0.25, 0.0)
    v_q1 = (lax.bitwise_and(lax.shift_right_logical(row32, 2), 3) + 1).astype(F32) * 0.25
    v_q2 = (lax.bitwise_and(row32, 3) + 1).astype(F32) * 0.25
    v_off = jnp.where(row32 >= 16, 0.25, 0.0)

    for copy in force_copies:
        copy.wait_recv()
    acc = mix(1, force_in, acc)
    for e in range(4):
        for c in range(3):
            row = 8 * c + 4 * (e % 2)
            value = acc[3 * e + c]
            moved[e // 2, row : row + 4] = (value + pltpu.roll(value, 4, 0))[0:4]
    moved_copy = pltpu.make_async_remote_copy(
        src_ref=moved.at[1 - half],
        dst_ref=moved_in,
        send_sem=moved_sem.at[0],
        recv_sem=moved_sem.at[1],
        device_id={"bead": 2 * ring + (1 - half)},
        device_id_type=MESH,
    )
    moved_copy.start()

    us, vs = [], []
    for e in range(4):
        u, v = [], []
        for blk in range(4):
            row = 4 * (e % 2) + blk
            x = moved[e // 2, row : row + 1]
            y = moved[e // 2, 8 + row : 9 + row]
            z = moved[e // 2, 16 + row : 17 + row]
            u.append(cos_turns(u_q * x - u_off))
            v.append(cos_turns(v_q1 * y + v_q2 * z - v_off))
        us.append(jnp.concatenate(u, axis=1))
        vs.append(jnp.concatenate(v, axis=1))
    raw = lax.dot_general(
        jnp.concatenate(us, axis=0),
        jnp.concatenate(vs, axis=0),
        (((1,), (1,)), ((), ())),
        precision=HIGHEST,
        preferred_element_type=F32,
    )
    raw = jnp.where(same_bead, raw, 0.0)
    by_q = jnp.dot(raw, choose, precision=HIGHEST, preferred_element_type=F32)
    parts = direct * by_q + crossed * pltpu.roll(by_q, 64, 1)
    me = N * half + space
    for e in range(4):
        sum_in[me, e : e + 1] = jnp.sum(parts[8 * e : 8 * e + 8], axis=0, keepdims=True)

    sum_copies = []
    for side in range(2):
        for step in (8, 9, 7, 10, 6, 11, 5, 12, 4, 13, 3, 14, 2, 15, 1, 0):
            if side == 0 and step == 0:
                continue
            copy = pltpu.make_async_remote_copy(
                src_ref=sum_in.at[me],
                dst_ref=sum_in.at[me],
                send_sem=sum_send.at[N * side + step],
                recv_sem=sum_recv.at[N * side + (N - step) % N],
                device_id=plane(side, step),
                device_id_type=MESH,
            )
            copy.start()
            sum_copies.append(copy)
    moved_copy.wait_recv()
    for part, rows in ((half, moved.at[half]), (1 - half, moved_in)):
        for c in range(3):
            for b in range(2):
                for blk in range(4):
                    at = pl.ds(pl.multiple_of(GHOST * part + 128 * blk, 128), 128)
                    row = 8 * c + 4 * b + blk
                    new_pos[c, b : b + 1, at] = rows[row : row + 1, :]
    dense_tiles(1, 3)
    for copy in sum_copies:
        copy.wait_recv()
    total = sum_in[0]
    for r in range(1, 2 * N):
        total = total + sum_in[r]
    all_in[0] = total
    all_copies = []
    for step in (4, 3, 5, 2, 6, 1, 7):
        copy = pltpu.make_async_remote_copy(
            src_ref=all_in.at[0],
            dst_ref=all_in.at[RING - step],
            send_sem=all_send.at[step],
            recv_sem=all_recv.at[RING - step],
            device_id={"bead": 2 * lax.rem(ring + step, RING) + half},
            device_id_type=MESH,
        )
        copy.start()
        all_copies.append(copy)
    dense_tiles(3, 4)
    for copy in all_copies:
        copy.wait_recv()
    every = jnp.concatenate([all_in[r] for r in range(RING)], axis=0)
    for b in range(2):
        own = jnp.where(half == 0, every[b : b + 1], every[2 + b : 3 + b])
        prod = every * (own * (1.0 / (APD * N)))
        prod = prod + pltpu.roll(prod, 64, 1)
        low = prod if b == 0 else jnp.concatenate([prod[b:], prod[0:b]], axis=0)
        high = jnp.concatenate([prod[b + 2 :], prod[0 : b + 2]], axis=0)
        corr[b] = jnp.where(half == 0, low, high)[:, 0:64]

    for copy in small + ghosts + pos_copies + force_copies + [moved_copy] + sum_copies + all_copies:
        copy.wait_send()


def write_out(feats_in, pos_in, corr_in, feats_out, pos_out, corr_out, sems):
    copies = []
    for source, target in ((feats_in, feats_out), (pos_in, pos_out), (corr_in, corr_out)):
        copy = pltpu.make_async_copy(source, target, sems.at[len(copies)])
        copy.start()
        copies.append(copy)
    for copy in copies:
        copy.wait()


def on_device(
    features, positions, send_rows, neighbours, nbr_mask, w_pair, w_in, w_out, omega, q_index
):
    vmem = pl.BlockSpec(memory_space=pltpu.VMEM)
    hbm = pl.BlockSpec(memory_space=pltpu.HBM)
    dma = pltpu.SemaphoreType.DMA
    shapes = (
        jax.ShapeDtypeStruct((2, APD, W), BF16),
        jax.ShapeDtypeStruct((3, 2, APD), F32),
        jax.ShapeDtypeStruct((2, 32, 64), F32),
    )
    results = pl.pallas_call(
        kernel,
        out_shape=shapes,
        in_specs=[hbm] * 10,
        out_specs=(vmem, vmem, vmem),
        scratch_shapes=[
            pltpu.VMEM((2, APD, W), BF16),
            pltpu.VMEM((3, 2, APD), F32),
            pltpu.VMEM((1, 2, GHOST), jnp.int32),
            pltpu.VMEM((SLOTS, APD), jnp.int32),
            pltpu.VMEM((SLOTS, APD), jnp.int32),
            pltpu.VMEM((1, W), BF16),
            pltpu.VMEM((2 * W, 512), BF16),
            pltpu.VMEM((512, W), BF16),
            pltpu.SMEM((2,), F32),
            pltpu.VMEM((3, 64), jnp.int32),
            dma((10,)),
            pltpu.VMEM((8, EXT), F32),
            pltpu.VMEM((2, 8, GHOST), F32),
            pltpu.VMEM((2, 2, GHOST, W), BF16),
            pltpu.VMEM((2, 2, GHOST, W), BF16),
            pltpu.VMEM((APD, 128), F32),
            pltpu.VMEM((2, TILE, EXT), BF16),
            pltpu.VMEM((2, 32, 128), F32),
            pltpu.VMEM((N, 32, 128), F32),
            pltpu.VMEM((2, 24, 128), F32),
            pltpu.VMEM((N, 24, 128), F32),
            pltpu.VMEM((2, 32, 128), F32),
            pltpu.VMEM((128, 1024), F32),
            pltpu.VMEM((2, 24, 128), F32),
            pltpu.VMEM((24, 128), F32),
            pltpu.VMEM((2 * N, 4, 128), F32),
            pltpu.VMEM((RING, 4, 128), F32),
            dma((2,)),
            dma((2,)),
            dma((2,)),
            dma((2,)),
            dma((N,)),
            dma((N,)),
            dma((N,)),
            dma((N,)),
            dma((2,)),
            dma((2 * N,)),
            dma((2 * N,)),
            dma((RING,)),
            dma((RING,)),
        ],
        compiler_params=pltpu.CompilerParams(
            collective_id=0, has_side_effects=True, vmem_limit_bytes=64 * 2**20 - 2**17
        ),
    )(
        features,
        jnp.transpose(positions, (1, 0, 2)),
        send_rows,
        neighbours,
        nbr_mask,
        w_pair.reshape(1, W),
        w_in,
        w_out,
        omega,
        q_index,
    )
    new_features, new_positions, correlation = pl.pallas_call(
        write_out,
        out_shape=shapes,
        in_specs=[vmem] * 3,
        out_specs=(hbm, hbm, hbm),
        scratch_shapes=[dma((3,))],
    )(*results)
    return (new_features, jnp.transpose(new_positions, (1, 0, 2)), correlation)


def solution(mesh):
    in_specs = (
        P("bead", "space", None),
        P("bead", None, "space"),
        P("space", None, None),
        P(None, "space"),
        P(None, "space"),
        P(),
        P(),
        P(),
        P("bead"),
        P(),
    )
    out_specs = (P("bead", "space", None), P("bead", None, "space"), P("bead", None, None))
    return jax.shard_map(
        on_device, mesh=mesh, in_specs=in_specs, out_specs=out_specs, check_vma=False
    )
```

time: 54 us -> 47.9 us (0.89)
  local copies, waits for them, and re-layouts: 8.19 us -> 0 us
  Pallas kernels: 44.7 us -> 47.1 us
    unnamed x25 -> x0, local copies, waits for them, and re-layouts: 7.56 us -> none
    pallas_call x1 -> x2, Pallas kernels: 44.7 us -> 47.1 us  [the longest x1 45.2 us: on_device(): pl.pallas_call(kernel, out_shape=shapes, in_specs=[hbm] * 10, out_specs=(...]
    pallas_call x1 -> x0, local copies, waits for them, and re-layouts: 0.63 us -> none  [on_device(): pl.pallas_call(kernel, out_shape=(jax.ShapeDtypeStruct((2, APD, W), BF16)...]
where the time goes in v2:
time: 47.9 us; the launch traced here: 47.8 us
  Pallas kernels  47.1 us (98%)
  between operations  0.64 us (1%)
    pallas_call x1, Pallas kernels, on_device(): pl.pallas_call(kernel, out_shape=shapes, in_specs=[hbm] * 10, out_specs=(...  45.2 us
    pallas_call x1, Pallas kernels, on_device(): pl.pallas_call(write_out, out_shape=shapes, in_specs=[vmem] * 3, out_spec...  1.88 us

profile of v2, /device:TPU:1, one launch (start us, length us, event | category | flops | bytes accessed | tf_op | source)
XLA Modules:
  0.0 47.8 jit_solution(605559500570466703)
XLA Ops:
  0.6 45.2 %shard_map.121 = (bf16[2,1024,128]{2,1,0:T(8,128)(2,1)}, f32[3,2,1024]{2,1,0:T(2,128)}, f32[2,32,64]{2,1,0:T(8,128)}) custom-call(bf16[2,1024,128]{2,1,0:T(8,128)(2,1)} %feats_hbm.1, f32[3,2,1024]{2,1,0:T(2,128)} %bitcast.3, s32[1,2,512]{2,1,0:T(2,128)} %send_hbm.1, s32[8,1024]{1,0:T(8,128)} %nbr_hbm.1, s32[8,1024]{1,0:T(8,128)} %mask_hbm.1, ...), custom_call_target="tpu_custom_call" | custom-call | tf_op jit(solution)/shard_map/pallas_call | solution.py:526
  45.9 1.9 %shard_map.122 = (bf16[2,1024,128]{2,1,0:T(8,128)(2,1)}, f32[3,2,1024]{2,1,0:T(2,128)}, f32[2,32,64]{2,1,0:T(8,128)}) custom-call(bf16[2,1024,128]{2,1,0:T(8,128)(2,1)} %get-tuple-element.9.feats_in, f32[3,2,1024]{2,1,0:T(2,128)} %get-tuple-element.10.pos_in, f32[2,32,64]{2,1,0:T(8,128)} %get-tuple-element.11.corr_in), custom_call_target="tpu_custom_call" | custom-call | tf_op jit(solution)/shard_map/pallas_call | solution.py:588

commit v3 on v2

--- a/solution.py
+++ b/solution.py
@@ -56,9 +56,9 @@
     w_out_hbm,
     omega_hbm,
     q_hbm,
-    new_feats,
-    new_pos,
-    corr,
+    feats_hbm_out,
+    pos_hbm_out,
+    corr_hbm_out,
     feats,
     pos,
     send,
@@ -70,11 +70,16 @@
     omega,
     q_index,
     load_sem,
+    new_feats,
+    new_pos,
+    corr,
+    store_sem,
     table,
     small_out,
     ghost_out,
-    ghost_in,
-    columns,
+    wide_feats,
+    picks,
+    terms,
     dense,
     pos_out,
     pos_in,
@@ -112,16 +117,6 @@
             "space": lax.rem(space + step, N),
         }
 
-    for step in (1, N - 1) + tuple(range(2, N - 1)):
-        pl.semaphore_signal(barrier, inc=1, device_id=plane(0, step), device_id_type=MESH)
-    for step in range(N):
-        pl.semaphore_signal(barrier, inc=1, device_id=plane(1, step), device_id_type=MESH)
-    for step in range(1, RING):
-        for side in range(2):
-            to = 2 * lax.rem(ring + step, RING) + side
-            pl.semaphore_signal(barrier, inc=1, device_id={"bead": to}, device_id_type=MESH)
-    partners = (N - 1) + N + 2 * (RING - 1)
-
     loads = []
     for source, target in (
         (w_pair_hbm, w_pair),
@@ -139,7 +134,15 @@
         copy.start()
         loads.append(copy)
 
-    lane = lax.broadcasted_iota(jnp.int32, (8, 128), 1)
+    for step in (1, N - 1) + tuple(range(2, N - 1)):
+        pl.semaphore_signal(barrier, inc=1, device_id=plane(0, step), device_id_type=MESH)
+    for step in range(N):
+        pl.semaphore_signal(barrier, inc=1, device_id=plane(1, step), device_id_type=MESH)
+    for step in range(1, RING):
+        for side in range(2):
+            to = 2 * lax.rem(ring + step, RING) + side
+            pl.semaphore_signal(barrier, inc=1, device_id={"bead": to}, device_id_type=MESH)
+    partners = (N - 1) + N + 2 * (RING - 1)
 
     for i in range(4):
         loads[i].wait()
@@ -221,38 +224,58 @@
     pos_copies = to_beads(pos_out, pos_in, pos_send, pos_recv, crossing + straight)
     pos_in[bead] = pos_out[half]
 
-    both = jnp.concatenate([feats[0], feats[1]], axis=1)
-    wide = lax.broadcasted_iota(jnp.int32, (128, APD), 1)
+    for b in range(2):
+        for blk in range(APD // 128):
+            at = slice(128 * blk, 128 * blk + 128)
+            wide_feats[W * b : W * b + W, at] = jnp.transpose(feats[b, at, :])
+    tall = lax.broadcasted_iota(jnp.int32, (APD, GHOST), 0)
     ghosts = []
     for side in range(2):
-        for blk in range(4):
-            idx = jnp.broadcast_to(
-                send[0, side : side + 1, 128 * blk : 128 * blk + 128], (128, 128)
+        hot = (tall == send[0, side : side + 1, :]).astype(F32).astype(BF16)
+        ghost_out[side] = jnp.dot(
+            wide_feats[:, 0:APD], hot, preferred_element_type=F32
+        ).astype(BF16)
+        start = APD + GHOST if side == 0 else APD
+        ghosts.append(
+            to_neighbour(
+                ghost_out.at[side],
+                wide_feats.at[:, pl.ds(start, GHOST)],
+                ghost_send,
+                ghost_recv,
+                side,
             )
-            col = jnp.transpose(idx)[:, 0:1]
-            hot = (col == wide).astype(F32).astype(BF16)
-            rows = jnp.dot(hot, both, preferred_element_type=F32).astype(BF16)
-            ghost_out[side, 0, 128 * blk : 128 * blk + 128] = rows[:, 0:W]
-            ghost_out[side, 1, 128 * blk : 128 * blk + 128] = rows[:, W:]
-        ghosts.append(
-            to_neighbour(ghost_out.at[side], ghost_in.at[1 - side], ghost_send, ghost_recv, side)
         )
+
+    def pick(at, picked, first, last):
+        idx = nbr[:, at]
+        hi = lax.shift_right_logical(idx, 7)
+        lo = lax.bitwise_and(idx, 127)
+        for h in range(first, last):
+            hit = hi == h
+            for q in range(8):
+                row = jnp.broadcast_to(table[q : q + 1, 128 * h : 128 * h + 128], (8, 128))
+                picked[q] = jnp.where(hit, lane_gather(row, lo), picked[q])
+        return picked
+
+    def own_block(blk, _):
+        at = pl.ds(pl.multiple_of(128 * blk, 128), 128)
+        got = pick(at, [jnp.zeros((8, 128), F32) for _ in range(8)], 0, APD // 128)
+        for q in range(8):
+            picks[q, :, at] = got[q]
+        return 0
+
+    lax.fori_loop(0, APD // 128, own_block, 0)
 
     for copy in small:
         copy.wait_recv()
 
     def block(part, blk):
         at = pl.ds(pl.multiple_of(GHOST * part + 128 * blk, 128), 128)
+        picked = pick(at, [picks[q, :, at] for q in range(8)], APD // 128, EXT // 128)
         idx = nbr[:, at]
         live = mask[:, at].astype(F32)
         hi = lax.shift_right_logical(idx, 7)
         lo = lax.bitwise_and(idx, 127)
-        picked = [jnp.zeros((8, 128), F32) for _ in range(8)]
-        for h in range(EXT // 128):
-            hit = hi == h
-            for q in range(8):
-                row = jnp.broadcast_to(table[q : q + 1, 128 * h : 128 * h + 128], (8, 128))
-                picked[q] = jnp.where(hit, lane_gather(row, lo), picked[q])
         code = (128 + lo).astype(F32) * lax.shift_left(jnp.ones_like(hi), hi).astype(F32)
         cs = []
         for b in range(2):
@@ -277,8 +300,9 @@
             same = pltpu.roll(idx, r, 0) == idx
             for b in range(2):
                 total[b] = total[b] + jnp.where(same, pltpu.roll(cs[b], r, 0), 0.0)
-        stack = jnp.concatenate([code, total[0], total[1], jnp.zeros((104, 128), F32)], axis=0)
-        columns[at, :] = jnp.transpose(stack)
+        terms[0, :, at] = code
+        terms[1, :, at] = total[0]
+        terms[2, :, at] = total[1]
 
     def blocks(part):
         def step(blk, _):
@@ -331,40 +355,38 @@
     for copy in ghosts:
         copy.wait_recv()
 
-    lane_code = (128 + lax.broadcasted_iota(jnp.int32, (16, 128), 1)).astype(F32)
+    sub_code = (128 + lax.broadcasted_iota(jnp.int32, (16, 128), 0)).astype(F32)
 
     def dense_tile(t):
-        def strip(s, _):
-            at = pl.ds(pl.multiple_of(t * TILE + s * 16, 16), 16)
-            cols = columns[at, :]
-
-            def spread_lane(j):
-                return jnp.broadcast_to(cols[:, j : j + 1], (16, 128)).astype(BF16)
-
-            codes = [spread_lane(k) for k in range(SLOTS)]
-            c0 = [spread_lane(8 + k) for k in range(SLOTS)]
-            c1 = [spread_lane(16 + k) for k in range(SLOTS)]
-            row = pl.ds(pl.multiple_of(s * 16, 16), 16)
-            for h in range(EXT // 128):
-                here = (lane_code * float(2**h)).astype(BF16)
-                a0 = jnp.zeros((16, 128), BF16)
-                a1 = jnp.zeros((16, 128), BF16)
-                for k in range(SLOTS):
-                    hit = codes[k] == here
-                    a0 = jnp.where(hit, c0[k], a0)
-                    a1 = jnp.where(hit, c1[k], a1)
-                dense[0, row, 128 * h : 128 * h + 128] = a0
-                dense[1, row, 128 * h : 128 * h + 128] = a1
-            return 0
-
-        lax.fori_loop(0, TILE // 16, strip, 0)
+        for blk in range(TILE // 128):
+            lanes = slice(128 * blk, 128 * blk + 128)
+            at = pl.ds(pl.multiple_of(t * TILE + 128 * blk, 128), 128)
+
+            def spread_row(kind, k):
+                return jnp.broadcast_to(terms[kind, k : k + 1, at], (16, 128)).astype(BF16)
+
+            codes, c0, c1 = [[spread_row(kind, k) for k in range(SLOTS)] for kind in range(3)]
+
+            def strip(s, _):
+                base = sub_code + (16 * s).astype(F32)
+                for h in range(EXT // 128):
+                    here = (base * float(2**h)).astype(BF16)
+                    a0 = jnp.zeros((16, 128), BF16)
+                    a1 = jnp.zeros((16, 128), BF16)
+                    for k in range(SLOTS):
+                        hit = codes[k] == here
+                        a0 = jnp.where(hit, c0[k], a0)
+                        a1 = jnp.where(hit, c1[k], a1)
+                    row = pl.ds(pl.multiple_of(128 * h + 16 * s, 16), 16)
+                    dense[0, row, lanes] = a0
+                    dense[1, row, lanes] = a1
+                return 0
+
+            lax.fori_loop(0, 8, strip, 0)
         at = pl.ds(pl.multiple_of(t * TILE, TILE), TILE)
         for b in range(2):
-            agg = jnp.dot(dense[b, :, 0:APD], feats[b], preferred_element_type=F32)
-            agg += jnp.dot(
-                dense[b, :, APD : APD + GHOST], ghost_in[0, b], preferred_element_type=F32
-            )
-            agg += jnp.dot(dense[b, :, APD + GHOST :], ghost_in[1, b], preferred_element_type=F32)
+            agg = jnp.dot(wide_feats[W * b : W * b + W], dense[b], preferred_element_type=F32)
+            agg = jnp.transpose(agg)
             mine = feats[b, at, :]
             joined = jnp.concatenate([mine, agg.astype(BF16)], axis=1)
             x = jnp.dot(joined, w_in[...], preferred_element_type=F32)
@@ -379,7 +401,20 @@
 
         lax.fori_loop(first, last, step, 0)
 
-    dense_tiles(0, 1)
+    stores = []
+
+    def store(source, target):
+        copy = pltpu.make_async_copy(source, target, store_sem.at[len(stores)])
+        copy.start()
+        stores.append(copy)
+
+    def dense_rows(first, last):
+        dense_tiles(first, last)
+        for b in range(2):
+            rows = pl.ds(first * TILE, (last - first) * TILE)
+            store(new_feats.at[b, rows], feats_hbm_out.at[b, rows])
+
+    dense_rows(0, 2)
 
     q0 = q_index[0:1, :]
     pick = 4 * (q_index[1:2, :] - 1) + (q_index[2:3, :] - 1)
@@ -467,7 +502,8 @@
                     at = pl.ds(pl.multiple_of(GHOST * part + 128 * blk, 128), 128)
                     row = 8 * c + 4 * b + blk
                     new_pos[c, b : b + 1, at] = rows[row : row + 1, :]
-    dense_tiles(1, 3)
+    store(new_pos, pos_hbm_out)
+    dense_rows(2, 3)
     for copy in sum_copies:
         copy.wait_recv()
     total = sum_in[0]
@@ -486,7 +522,7 @@
         )
         copy.start()
         all_copies.append(copy)
-    dense_tiles(3, 4)
+    dense_rows(3, 4)
     for copy in all_copies:
         copy.wait_recv()
     every = jnp.concatenate([all_in[r] for r in range(RING)], axis=0)
@@ -498,8 +534,11 @@
         high = jnp.concatenate([prod[b + 2 :], prod[0 : b + 2]], axis=0)
         corr[b] = jnp.where(half == 0, low, high)[:, 0:64]
 
+    store(corr, corr_hbm_out)
     for copy in small + ghosts + pos_copies + force_copies + [moved_copy] + sum_copies + all_copies:
         copy.wait_send()
+    for copy in stores:
+        copy.wait()
 
 
 def write_out(feats_in, pos_in, corr_in, feats_out, pos_out, corr_out, sems):
@@ -515,7 +554,6 @@
 def on_device(
     features, positions, send_rows, neighbours, nbr_mask, w_pair, w_in, w_out, omega, q_index
 ):
-    vmem = pl.BlockSpec(memory_space=pltpu.VMEM)
     hbm = pl.BlockSpec(memory_space=pltpu.HBM)
     dma = pltpu.SemaphoreType.DMA
     shapes = (
@@ -527,7 +565,7 @@
         kernel,
         out_shape=shapes,
         in_specs=[hbm] * 10,
-        out_specs=(vmem, vmem, vmem),
+        out_specs=(hbm, hbm, hbm),
         scratch_shapes=[
             pltpu.VMEM((2, APD, W), BF16),
             pltpu.VMEM((3, 2, APD), F32),
@@ -540,12 +578,17 @@
             pltpu.SMEM((2,), F32),
             pltpu.VMEM((3, 64), jnp.int32),
             dma((10,)),
+            pltpu.VMEM((2, APD, W), BF16),
+            pltpu.VMEM((3, 2, APD), F32),
+            pltpu.VMEM((2, 32, 64), F32),
+            dma((8,)),
             pltpu.VMEM((8, EXT), F32),
             pltpu.VMEM((2, 8, GHOST), F32),
-            pltpu.VMEM((2, 2, GHOST, W), BF16),
-            pltpu.VMEM((2, 2, GHOST, W), BF16),
-            pltpu.VMEM((APD, 128), F32),
-            pltpu.VMEM((2, TILE, EXT), BF16),
+            pltpu.VMEM((2, 2 * W, GHOST), BF16),
+            pltpu.VMEM((2 * W, EXT), BF16),
+            pltpu.VMEM((8, SLOTS, APD), F32),
+            pltpu.VMEM((3, SLOTS, APD), F32),
+            pltpu.VMEM((2, EXT, TILE), BF16),
             pltpu.VMEM((2, 32, 128), F32),
             pltpu.VMEM((N, 32, 128), F32),
             pltpu.VMEM((2, 24, 128), F32),
@@ -588,7 +631,7 @@
     new_features, new_positions, correlation = pl.pallas_call(
         write_out,
         out_shape=shapes,
-        in_specs=[vmem] * 3,
+        in_specs=[pl.BlockSpec(memory_space=pltpu.VMEM)] * 3,
         out_specs=(hbm, hbm, hbm),
         scratch_shapes=[dma((3,))],
     )(*results)

time: 47.9 us -> 43.3 us (0.904)
  Pallas kernels: 47.1 us -> 42.6 us
    pallas_call x1, Pallas kernels: 45.2 us -> 40.7 us  [on_device(): pl.pallas_call(kernel, out_shape=shapes, in_specs=[hbm] * 10, out_specs=(...]
where the time goes in v3:
time: 43.3 us; the launch traced here: 43.2 us
  Pallas kernels  42.6 us (98%)
  between operations  0.64 us (1%)
    pallas_call x1, Pallas kernels, on_device(): pl.pallas_call(kernel, out_shape=shapes, in_specs=[hbm] * 10, out_specs=(...  40.7 us
    pallas_call x1, Pallas kernels, on_device(): pl.pallas_call(write_out, out_shape=shapes, in_specs=[pl.BlockSpec(memory...  1.88 us

profile of v3, /device:TPU:1, one launch (start us, length us, event | category | flops | bytes accessed | tf_op | source)
XLA Modules:
  0.0 43.2 jit_solution(4786665690782515567)
XLA Ops:
  0.6 40.7 %shard_map.121 = (bf16[2,1024,128]{2,1,0:T(8,128)(2,1)}, f32[3,2,1024]{2,1,0:T(2,128)}, f32[2,32,64]{2,1,0:T(8,128)}) custom-call(bf16[2,1024,128]{2,1,0:T(8,128)(2,1)} %feats_hbm.1, f32[3,2,1024]{2,1,0:T(2,128)} %bitcast.3, s32[1,2,512]{2,1,0:T(2,128)} %send_hbm.1, s32[8,1024]{1,0:T(8,128)} %nbr_hbm.1, s32[8,1024]{1,0:T(8,128)} %mask_hbm.1, ...), custom_call_target="tpu_custom_call" | custom-call | tf_op jit(solution)/shard_map/pallas_call | solution.py:564
  41.3 1.9 %shard_map.122 = (bf16[2,1024,128]{2,1,0:T(8,128)(2,1)}, f32[3,2,1024]{2,1,0:T(2,128)}, f32[2,32,64]{2,1,0:T(8,128)}) custom-call(bf16[2,1024,128]{2,1,0:T(8,128)(2,1)} %get-tuple-element.9.feats_in, f32[3,2,1024]{2,1,0:T(2,128)} %get-tuple-element.10.pos_in, f32[2,32,64]{2,1,0:T(8,128)} %get-tuple-element.11.corr_in), custom_call_target="tpu_custom_call" | custom-call | tf_op jit(solution)/shard_map/pallas_call | solution.py:631

commit v4 on v3

--- a/solution.py
+++ b/solution.py
@@ -80,6 +80,7 @@
     wide_feats,
     picks,
     terms,
+    agg_own,
     dense,
     pos_out,
     pos_in,
@@ -229,22 +230,11 @@
             at = slice(128 * blk, 128 * blk + 128)
             wide_feats[W * b : W * b + W, at] = jnp.transpose(feats[b, at, :])
     tall = lax.broadcasted_iota(jnp.int32, (APD, GHOST), 0)
-    ghosts = []
     for side in range(2):
         hot = (tall == send[0, side : side + 1, :]).astype(F32).astype(BF16)
         ghost_out[side] = jnp.dot(
             wide_feats[:, 0:APD], hot, preferred_element_type=F32
         ).astype(BF16)
-        start = APD + GHOST if side == 0 else APD
-        ghosts.append(
-            to_neighbour(
-                ghost_out.at[side],
-                wide_feats.at[:, pl.ds(start, GHOST)],
-                ghost_send,
-                ghost_recv,
-                side,
-            )
-        )
 
     def pick(at, picked, first, last):
         idx = nbr[:, at]
@@ -316,6 +306,94 @@
     blocks(half)
     force_copies += to_beads(force_out, force_in, force_send, force_recv, straight)
     force_in[bead] = force_out[half]
+    ghosts = []
+    for side in range(2):
+        start = APD + GHOST if side == 0 else APD
+        ghosts.append(
+            to_neighbour(
+                ghost_out.at[side],
+                wide_feats.at[:, pl.ds(start, GHOST)],
+                ghost_send,
+                ghost_recv,
+                side,
+            )
+        )
+
+    sub_code = (128 + lax.broadcasted_iota(jnp.int32, (16, 128), 0)).astype(F32)
+
+    def dense_half(t, first):
+        for blk in range(TILE // 128):
+            lanes = slice(128 * blk, 128 * blk + 128)
+            at = pl.ds(pl.multiple_of(t * TILE + 128 * blk, 128), 128)
+
+            def spread_row(kind, k):
+                return jnp.broadcast_to(terms[kind, k : k + 1, at], (16, 128)).astype(BF16)
+
+            codes, c0, c1 = [[spread_row(kind, k) for k in range(SLOTS)] for kind in range(3)]
+
+            def strip(s, _):
+                base = sub_code + (16 * s).astype(F32)
+                for h in range(8):
+                    here = (base * float(2 ** (first // 128 + h))).astype(BF16)
+                    a0 = jnp.zeros((16, 128), BF16)
+                    a1 = jnp.zeros((16, 128), BF16)
+                    for k in range(SLOTS):
+                        hit = codes[k] == here
+                        a0 = jnp.where(hit, c0[k], a0)
+                        a1 = jnp.where(hit, c1[k], a1)
+                    row = pl.ds(pl.multiple_of(128 * h + 16 * s, 16), 16)
+                    dense[0, row, lanes] = a0
+                    dense[1, row, lanes] = a1
+                return 0
+
+            lax.fori_loop(0, 8, strip, 0)
+        return [
+            jnp.dot(
+                wide_feats[W * b : W * b + W, first : first + APD],
+                dense[b],
+                preferred_element_type=F32,
+            )
+            for b in range(2)
+        ]
+
+    def own_tile(t, _):
+        at = pl.ds(pl.multiple_of(t * TILE, TILE), TILE)
+        agg_own[0, :, at], agg_own[1, :, at] = dense_half(t, 0)
+        return 0
+
+    def dense_tile(t):
+        at = pl.ds(pl.multiple_of(t * TILE, TILE), TILE)
+        ghost_part = dense_half(t, APD)
+        for b in range(2):
+            agg = jnp.transpose(agg_own[b, :, at] + ghost_part[b])
+            mine = feats[b, at, :]
+            joined = jnp.concatenate([mine, agg.astype(BF16)], axis=1)
+            x = jnp.dot(joined, w_in[...], preferred_element_type=F32)
+            hidden = (x * (0.5 * (1.0 + jnp.tanh(0.5 * x)))).astype(BF16)
+            out = mine.astype(F32) + jnp.dot(hidden, w_out[...], preferred_element_type=F32)
+            new_feats[b, at, :] = out.astype(BF16)
+
+    def dense_tiles(first, last):
+        def step(t, _):
+            dense_tile(t)
+            return 0
+
+        lax.fori_loop(first, last, step, 0)
+
+    stores = []
+
+    def store(source, target):
+        copy = pltpu.make_async_copy(source, target, store_sem.at[len(stores)])
+        copy.start()
+        stores.append(copy)
+
+    def dense_rows(first, last):
+        dense_tiles(first, last)
+        for b in range(2):
+            rows = pl.ds(first * TILE, (last - first) * TILE)
+            store(new_feats.at[b, rows], feats_hbm_out.at[b, rows])
+
+    lax.fori_loop(0, APD // TILE, own_tile, 0)
 
     for copy in pos_copies:
         copy.wait_recv()
@@ -354,67 +432,6 @@
         loads[i].wait()
     for copy in ghosts:
         copy.wait_recv()
-
-    sub_code = (128 + lax.broadcasted_iota(jnp.int32, (16, 128), 0)).astype(F32)
-
-    def dense_tile(t):
-        for blk in range(TILE // 128):
-            lanes = slice(128 * blk, 128 * blk + 128)
-            at = pl.ds(pl.multiple_of(t * TILE + 128 * blk, 128), 128)
-
-            def spread_row(kind, k):
-                return jnp.broadcast_to(terms[kind, k : k + 1, at], (16, 128)).astype(BF16)
-
-            codes, c0, c1 = [[spread_row(kind, k) for k in range(SLOTS)] for kind in range(3)]
-
-            def strip(s, _):
-                base = sub_code + (16 * s).astype(F32)
-                for h in range(EXT // 128):
-                    here = (base * float(2**h)).astype(BF16)
-                    a0 = jnp.zeros((16, 128), BF16)
-                    a1 = jnp.zeros((16, 128), BF16)
-                    for k in range(SLOTS):
-                        hit = codes[k] == here
-                        a0 = jnp.where(hit, c0[k], a0)
-                        a1 = jnp.where(hit, c1[k], a1)
-                    row = pl.ds(pl.multiple_of(128 * h + 16 * s, 16), 16)
-                    dense[0, row, lanes] = a0
-                    dense[1, row, lanes] = a1
-                return 0
-
-            lax.fori_loop(0, 8, strip, 0)
-        at = pl.ds(pl.multiple_of(t * TILE, TILE), TILE)
-        for b in range(2):
-            agg = jnp.dot(wide_feats[W * b : W * b + W], dense[b], preferred_element_type=F32)
-            agg = jnp.transpose(agg)
-            mine = feats[b, at, :]
-            joined = jnp.concatenate([mine, agg.astype(BF16)], axis=1)
-            x = jnp.dot(joined, w_in[...], preferred_element_type=F32)
-            hidden = (x * (0.5 * (1.0 + jnp.tanh(0.5 * x)))).astype(BF16)
-            out = mine.astype(F32) + jnp.dot(hidden, w_out[...], preferred_element_type=F32)
-            new_feats[b, at, :] = out.astype(BF16)
-
-    def dense_tiles(first, last):
-        def step(t, _):
-            dense_tile(t)
-            return 0
-
-        lax.fori_loop(first, last, step, 0)
-
-    stores = []
-
-    def store(source, target):
-        copy = pltpu.make_async_copy(source, target, store_sem.at[len(stores)])
-        copy.start()
-        stores.append(copy)
-
-    def dense_rows(first, last):
-        dense_tiles(first, last)
-        for b in range(2):
-            rows = pl.ds(first * TILE, (last - first) * TILE)
-            store(new_feats.at[b, rows], feats_hbm_out.at[b, rows])
-
-    dense_rows(0, 2)
 
     q0 = q_index[0:1, :]
     pick = 4 * (q_index[1:2, :] - 1) + (q_index[2:3, :] - 1)
@@ -503,7 +520,7 @@
                     row = 8 * c + 4 * b + blk
                     new_pos[c, b : b + 1, at] = rows[row : row + 1, :]
     store(new_pos, pos_hbm_out)
-    dense_rows(2, 3)
+    dense_rows(0, 2)
     for copy in sum_copies:
         copy.wait_recv()
     total = sum_in[0]
@@ -522,7 +539,7 @@
         )
         copy.start()
         all_copies.append(copy)
-    dense_rows(3, 4)
+    dense_rows(2, 4)
     for copy in all_copies:
         copy.wait_recv()
     every = jnp.concatenate([all_in[r] for r in range(RING)], axis=0)
@@ -588,7 +605,8 @@
             pltpu.VMEM((2 * W, EXT), BF16),
             pltpu.VMEM((8, SLOTS, APD), F32),
             pltpu.VMEM((3, SLOTS, APD), F32),
-            pltpu.VMEM((2, EXT, TILE), BF16),
+            pltpu.VMEM((2, W, APD), F32),
+            pltpu.VMEM((2, APD, TILE), BF16),
             pltpu.VMEM((2, 32, 128), F32),
             pltpu.VMEM((N, 32, 128), F32),
             pltpu.VMEM((2, 24, 128), F32),

time: 43.3 us -> 40 us (0.924)
  Pallas kernels: 42.6 us -> 39.2 us
    pallas_call x1, Pallas kernels: 40.7 us -> 37.3 us  [on_device(): pl.pallas_call(kernel, out_shape=shapes, in_specs=[hbm] * 10, out_specs=(...]
where the time goes in v4:
time: 40 us; the launch traced here: 39.9 us
  Pallas kernels  39.2 us (98%)
  between operations  0.64 us (2%)
    pallas_call x1, Pallas kernels, on_device(): pl.pallas_call(kernel, out_shape=shapes, in_specs=[hbm] * 10, out_specs=(...  37.3 us
    pallas_call x1, Pallas kernels, on_device(): pl.pallas_call(write_out, out_shape=shapes, in_specs=[pl.BlockSpec(memory...  1.88 us

profile of v4, /device:TPU:1, one launch (start us, length us, event | category | flops | bytes accessed | tf_op | source)
XLA Modules:
  0.0 39.9 jit_solution(1364796377898614255)
XLA Ops:
  0.6 37.3 %shard_map.121 = (bf16[2,1024,128]{2,1,0:T(8,128)(2,1)}, f32[3,2,1024]{2,1,0:T(2,128)}, f32[2,32,64]{2,1,0:T(8,128)}) custom-call(bf16[2,1024,128]{2,1,0:T(8,128)(2,1)} %feats_hbm.1, f32[3,2,1024]{2,1,0:T(2,128)} %bitcast.3, s32[1,2,512]{2,1,0:T(2,128)} %send_hbm.1, s32[8,1024]{1,0:T(8,128)} %nbr_hbm.1, s32[8,1024]{1,0:T(8,128)} %mask_hbm.1, ...), custom_call_target="tpu_custom_call" | custom-call | tf_op jit(solution)/shard_map/pallas_call | solution.py:581
  38.0 1.9 %shard_map.122 = (bf16[2,1024,128]{2,1,0:T(8,128)(2,1)}, f32[3,2,1024]{2,1,0:T(2,128)}, f32[2,32,64]{2,1,0:T(8,128)}) custom-call(bf16[2,1024,128]{2,1,0:T(8,128)(2,1)} %get-tuple-element.9.feats_in, f32[3,2,1024]{2,1,0:T(2,128)} %get-tuple-element.10.pos_in, f32[2,32,64]{2,1,0:T(8,128)} %get-tuple-element.11.corr_in), custom_call_target="tpu_custom_call" | custom-call | tf_op jit(solution)/shard_map/pallas_call | solution.py:649

commit v5 on v4

--- a/solution.py
+++ b/solution.py
@@ -319,7 +319,7 @@
             )
         )
 
-    sub_code = (128 + lax.broadcasted_iota(jnp.int32, (16, 128), 0)).astype(F32)
+    sub_code = (128 + lax.broadcasted_iota(jnp.int32, (32, 128), 0)).astype(F32)
 
     def dense_half(t, first):
         for blk in range(TILE // 128):
@@ -327,26 +327,26 @@
             at = pl.ds(pl.multiple_of(t * TILE + 128 * blk, 128), 128)
 
             def spread_row(kind, k):
-                return jnp.broadcast_to(terms[kind, k : k + 1, at], (16, 128)).astype(BF16)
+                return jnp.broadcast_to(terms[kind, k : k + 1, at], (32, 128)).astype(BF16)
 
             codes, c0, c1 = [[spread_row(kind, k) for k in range(SLOTS)] for kind in range(3)]
 
             def strip(s, _):
-                base = sub_code + (16 * s).astype(F32)
+                base = sub_code + (32 * s).astype(F32)
                 for h in range(8):
                     here = (base * float(2 ** (first // 128 + h))).astype(BF16)
-                    a0 = jnp.zeros((16, 128), BF16)
-                    a1 = jnp.zeros((16, 128), BF16)
+                    a0 = jnp.zeros((32, 128), BF16)
+                    a1 = jnp.zeros((32, 128), BF16)
                     for k in range(SLOTS):
                         hit = codes[k] == here
                         a0 = jnp.where(hit, c0[k], a0)
                         a1 = jnp.where(hit, c1[k], a1)
-                    row = pl.ds(pl.multiple_of(128 * h + 16 * s, 16), 16)
+                    row = pl.ds(pl.multiple_of(128 * h + 32 * s, 32), 32)
                     dense[0, row, lanes] = a0
                     dense[1, row, lanes] = a1
                 return 0
 
-            lax.fori_loop(0, 8, strip, 0)
+            lax.fori_loop(0, 4, strip, 0)
         return [
             jnp.dot(
                 wide_feats[W * b : W * b + W, first : first + APD],
@@ -430,8 +430,6 @@
 
     for i in range(7, 10):
         loads[i].wait()
-    for copy in ghosts:
-        copy.wait_recv()
 
     q0 = q_index[0:1, :]
     pick = 4 * (q_index[1:2, :] - 1) + (q_index[2:3, :] - 1)
@@ -497,7 +495,7 @@
         sum_in[me, e : e + 1] = jnp.sum(parts[8 * e : 8 * e + 8], axis=0, keepdims=True)
 
     sum_copies = []
-    for side in range(2):
+    for side in (1, 0):
         for step in (8, 9, 7, 10, 6, 11, 5, 12, 4, 13, 3, 14, 2, 15, 1, 0):
             if side == 0 and step == 0:
                 continue
@@ -520,6 +518,8 @@
                     row = 8 * c + 4 * b + blk
                     new_pos[c, b : b + 1, at] = rows[row : row + 1, :]
     store(new_pos, pos_hbm_out)
+    for copy in ghosts:
+        copy.wait_recv()
     dense_rows(0, 2)
     for copy in sum_copies:
         copy.wait_recv()

time: 40 us -> 39.2 us (0.980)
  Pallas kernels: 39.2 us -> 38.4 us
    pallas_call x1, Pallas kernels: 37.3 us -> 36.5 us  [on_device(): pl.pallas_call(kernel, out_shape=shapes, in_specs=[hbm] * 10, out_specs=(...]
where the time goes in v5:
time: 39.2 us; the launch traced here: 39.1 us
  Pallas kernels  38.4 us (98%)
  between operations  0.64 us (2%)
    pallas_call x1, Pallas kernels, on_device(): pl.pallas_call(kernel, out_shape=shapes, in_specs=[hbm] * 10, out_specs=(...  36.5 us
    pallas_call x1, Pallas kernels, on_device(): pl.pallas_call(write_out, out_shape=shapes, in_specs=[pl.BlockSpec(memory...  1.88 us

profile of v5, /device:TPU:1, one launch (start us, length us, event | category | flops | bytes accessed | tf_op | source)
XLA Modules:
  0.0 39.1 jit_solution(7464112323029201651)
XLA Ops:
  0.6 36.5 %shard_map.121 = (bf16[2,1024,128]{2,1,0:T(8,128)(2,1)}, f32[3,2,1024]{2,1,0:T(2,128)}, f32[2,32,64]{2,1,0:T(8,128)}) custom-call(bf16[2,1024,128]{2,1,0:T(8,128)(2,1)} %feats_hbm.1, f32[3,2,1024]{2,1,0:T(2,128)} %bitcast.3, s32[1,2,512]{2,1,0:T(2,128)} %send_hbm.1, s32[8,1024]{1,0:T(8,128)} %nbr_hbm.1, s32[8,1024]{1,0:T(8,128)} %mask_hbm.1, ...), custom_call_target="tpu_custom_call" | custom-call | tf_op jit(solution)/shard_map/pallas_call | solution.py:581
  37.2 1.9 %shard_map.122 = (bf16[2,1024,128]{2,1,0:T(8,128)(2,1)}, f32[3,2,1024]{2,1,0:T(2,128)}, f32[2,32,64]{2,1,0:T(8,128)}) custom-call(bf16[2,1024,128]{2,1,0:T(8,128)(2,1)} %get-tuple-element.9.feats_in, f32[3,2,1024]{2,1,0:T(2,128)} %get-tuple-element.10.pos_in, f32[2,32,64]{2,1,0:T(8,128)} %get-tuple-element.11.corr_in), custom_call_target="tpu_custom_call" | custom-call | tf_op jit(solution)/shard_map/pallas_call | solution.py:649

commit v6 on v5

--- a/solution.py
+++ b/solution.py
@@ -262,11 +262,7 @@
     def block(part, blk):
         at = pl.ds(pl.multiple_of(GHOST * part + 128 * blk, 128), 128)
         picked = pick(at, [picks[q, :, at] for q in range(8)], APD // 128, EXT // 128)
-        idx = nbr[:, at]
         live = mask[:, at].astype(F32)
-        hi = lax.shift_right_logical(idx, 7)
-        lo = lax.bitwise_and(idx, 127)
-        code = (128 + lo).astype(F32) * lax.shift_left(jnp.ones_like(hi), hi).astype(F32)
         cs = []
         for b in range(2):
             d = []
@@ -285,14 +281,8 @@
                 row = pl.ds(8 * c + 4 * b + blk, 1)
                 force_out[part, row, :] = jnp.sum(pair * d[c], axis=0, keepdims=True)
             cs.append(weight)
-        total = list(cs)
-        for r in range(1, SLOTS):
-            same = pltpu.roll(idx, r, 0) == idx
-            for b in range(2):
-                total[b] = total[b] + jnp.where(same, pltpu.roll(cs[b], r, 0), 0.0)
-        terms[0, :, at] = code
-        terms[1, :, at] = total[0]
-        terms[2, :, at] = total[1]
+        terms[1, :, at] = cs[0]
+        terms[2, :, at] = cs[1]
 
     def blocks(part):
         def step(blk, _):
@@ -318,6 +308,26 @@
                 side,
             )
         )
+
+    def merge(blk, _):
+        at = pl.ds(pl.multiple_of(128 * blk, 128), 128)
+        idx = nbr[:, at]
+        hi = lax.shift_right_logical(idx, 7)
+        lo = lax.bitwise_and(idx, 127)
+        terms[0, :, at] = (128 + lo).astype(F32) * lax.shift_left(
+            jnp.ones_like(hi), hi
+        ).astype(F32)
+        single = [terms[1 + b, :, at] for b in range(2)]
+        total = list(single)
+        for r in range(1, SLOTS):
+            same = pltpu.roll(idx, r, 0) == idx
+            for b in range(2):
+                total[b] = total[b] + jnp.where(same, pltpu.roll(single[b], r, 0), 0.0)
+        for b in range(2):
+            terms[1 + b, :, at] = total[b]
+        return 0
+
+    lax.fori_loop(0, APD // 128, merge, 0)
 
     sub_code = (128 + lax.broadcasted_iota(jnp.int32, (32, 128), 0)).astype(F32)
 
@@ -480,11 +490,15 @@
             v.append(cos_turns(v_q1 * y + v_q2 * z - v_off))
         us.append(jnp.concatenate(u, axis=1))
         vs.append(jnp.concatenate(v, axis=1))
+    u = jnp.concatenate(us, axis=0)
+    v = jnp.concatenate(vs, axis=0)
+    u_high, v_high = u.astype(BF16), v.astype(BF16)
+    u_low = (u - u_high.astype(F32)).astype(BF16)
+    v_low = (v - v_high.astype(F32)).astype(BF16)
     raw = lax.dot_general(
-        jnp.concatenate(us, axis=0),
-        jnp.concatenate(vs, axis=0),
+        jnp.concatenate([u_high, u_high, u_low], axis=1),
+        jnp.concatenate([v_high, v_low, v_high], axis=1),
         (((1,), (1,)), ((), ())),
-        precision=HIGHEST,
         preferred_element_type=F32,
     )
     raw = jnp.where(same_bead, raw, 0.0)

time: 39.2 us -> 39.2 us (level)
  no operation moved by 1% of the time
where the time goes in v6:
time: 39.2 us; the launch traced here: 38.9 us
  Pallas kernels  38.3 us (98%)
  between operations  0.64 us (2%)
    pallas_call x1, Pallas kernels, on_device(): pl.pallas_call(kernel, out_shape=shapes, in_specs=[hbm] * 10, out_specs=(...  36.4 us
    pallas_call x1, Pallas kernels, on_device(): pl.pallas_call(write_out, out_shape=shapes, in_specs=[pl.BlockSpec(memory...  1.88 us

profile of v6, /device:TPU:1, one launch (start us, length us, event | category | flops | bytes accessed | tf_op | source)
XLA Modules:
  0.0 38.9 jit_solution(17747190070941681187)
XLA Ops:
  0.6 36.4 %shard_map.121 = (bf16[2,1024,128]{2,1,0:T(8,128)(2,1)}, f32[3,2,1024]{2,1,0:T(2,128)}, f32[2,32,64]{2,1,0:T(8,128)}) custom-call(bf16[2,1024,128]{2,1,0:T(8,128)(2,1)} %feats_hbm.1, f32[3,2,1024]{2,1,0:T(2,128)} %bitcast.3, s32[1,2,512]{2,1,0:T(2,128)} %send_hbm.1, s32[8,1024]{1,0:T(8,128)} %nbr_hbm.1, s32[8,1024]{1,0:T(8,128)} %mask_hbm.1, ...), custom_call_target="tpu_custom_call" | custom-call | tf_op jit(solution)/shard_map/pallas_call | solution.py:595
  37.1 1.9 %shard_map.122 = (bf16[2,1024,128]{2,1,0:T(8,128)(2,1)}, f32[3,2,1024]{2,1,0:T(2,128)}, f32[2,32,64]{2,1,0:T(8,128)}) custom-call(bf16[2,1024,128]{2,1,0:T(8,128)(2,1)} %get-tuple-element.9.feats_in, f32[3,2,1024]{2,1,0:T(2,128)} %get-tuple-element.10.pos_in, f32[2,32,64]{2,1,0:T(8,128)} %get-tuple-element.11.corr_in), custom_call_target="tpu_custom_call" | custom-call | tf_op jit(solution)/shard_map/pallas_call | solution.py:663

commit v7 on v6

--- a/solution.py
+++ b/solution.py
@@ -374,14 +374,18 @@
     def dense_tile(t):
         at = pl.ds(pl.multiple_of(t * TILE, TILE), TILE)
         ghost_part = dense_half(t, APD)
+        mine = jnp.concatenate([feats[b, at, :] for b in range(2)], axis=0)
+        agg = jnp.concatenate(
+            [jnp.transpose(agg_own[b, :, at] + ghost_part[b]).astype(BF16) for b in range(2)],
+            axis=0,
+        )
+        x = jnp.dot(
+            jnp.concatenate([mine, agg], axis=1), w_in[...], preferred_element_type=F32
+        )
+        hidden = (x * (0.5 * (1.0 + jnp.tanh(0.5 * x)))).astype(BF16)
+        out = mine.astype(F32) + jnp.dot(hidden, w_out[...], preferred_element_type=F32)
         for b in range(2):
-            agg = jnp.transpose(agg_own[b, :, at] + ghost_part[b])
-            mine = feats[b, at, :]
-            joined = jnp.concatenate([mine, agg.astype(BF16)], axis=1)
-            x = jnp.dot(joined, w_in[...], preferred_element_type=F32)
-            hidden = (x * (0.5 * (1.0 + jnp.tanh(0.5 * x)))).astype(BF16)
-            out = mine.astype(F32) + jnp.dot(hidden, w_out[...], preferred_element_type=F32)
-            new_feats[b, at, :] = out.astype(BF16)
+            new_feats[b, at, :] = out[TILE * b : TILE * b + TILE].astype(BF16)
 
     def dense_tiles(first, last):
         def step(t, _):

time: 39.2 us -> 39.1 us (level)
  no operation moved by 1% of the time
where the time goes in v7:
time: 39.1 us; the launch traced here: 38.9 us
  Pallas kernels  38.3 us (98%)
  between operations  0.64 us (2%)
    pallas_call x1, Pallas kernels, on_device(): pl.pallas_call(kernel, out_shape=shapes, in_specs=[hbm] * 10, out_specs=(...  36.4 us
    pallas_call x1, Pallas kernels, on_device(): pl.pallas_call(write_out, out_shape=shapes, in_specs=[pl.BlockSpec(memory...  1.88 us

profile of v7, /device:TPU:1, one launch (start us, length us, event | category | flops | bytes accessed | tf_op | source)
XLA Modules:
  0.0 38.9 jit_solution(17138415864278911912)
XLA Ops:
  0.6 36.4 %shard_map.121 = (bf16[2,1024,128]{2,1,0:T(8,128)(2,1)}, f32[3,2,1024]{2,1,0:T(2,128)}, f32[2,32,64]{2,1,0:T(8,128)}) custom-call(bf16[2,1024,128]{2,1,0:T(8,128)(2,1)} %feats_hbm.1, f32[3,2,1024]{2,1,0:T(2,128)} %bitcast.3, s32[1,2,512]{2,1,0:T(2,128)} %send_hbm.1, s32[8,1024]{1,0:T(8,128)} %nbr_hbm.1, s32[8,1024]{1,0:T(8,128)} %mask_hbm.1, ...), custom_call_target="tpu_custom_call" | custom-call | tf_op jit(solution)/shard_map/pallas_call | solution.py:599
  37.1 1.9 %shard_map.122 = (bf16[2,1024,128]{2,1,0:T(8,128)(2,1)}, f32[3,2,1024]{2,1,0:T(2,128)}, f32[2,32,64]{2,1,0:T(8,128)}) custom-call(bf16[2,1024,128]{2,1,0:T(8,128)(2,1)} %get-tuple-element.9.feats_in, f32[3,2,1024]{2,1,0:T(2,128)} %get-tuple-element.10.pos_in, f32[2,32,64]{2,1,0:T(8,128)} %get-tuple-element.11.corr_in), custom_call_target="tpu_custom_call" | custom-call | tf_op jit(solution)/shard_map/pallas_call | solution.py:667
